TPU v7x, 128 devices: a whole 4x4x4 slice. The times are simulated.
128 devices in a mesh: ctx: 8 (over x, z_lo), exp: 16 (over z_hi, y, core).
Axes of the slice: x: 4, y: 4, z: 4 (z_hi: 2, z_lo: 2; z = z_hi * 2 + z_lo), core: 2. Of those that a mesh axis runs over, the one named last changes fastest.
Arguments:
- queries: bfloat16 [4, 2048, 4096], P(None, 'ctx', 'exp'), may hold values from -8 to 8
- keys: bfloat16 [4, 2048, 256], P(None, 'ctx'), may hold values from -8 to 8
- values: bfloat16 [4, 2048, 256], P(None, 'ctx'), may hold values from -6 to 6
- residual: bfloat16 [2048, 4, 4096], P(('ctx', 'exp')), may hold values from -6 to 6
- out_weight: bfloat16 [4096, 4096], P('exp'), may hold values from -0.09375 to 0.09375
- norm_gain: float32 [4096], replicated, may hold values from 0.1 to 1.9
- expert_ids: int32 [2048, 4, 8], P(('ctx', 'exp')), may hold values from 0 to 127, all different within a row; in each aligned block of 64 rows (0 to 63, 64 to 127, ..., all dimensions but the last counted through in order) at most 4 rows name the same one
- expert_gates: float32 [2048, 4, 8], P(('ctx', 'exp')), may hold values from 0.2 to 1
- w_gate: bfloat16 [128, 4096, 768], P(('ctx', 'exp')), may hold values from -0.09375 to 0.09375
- w_up: bfloat16 [128, 4096, 768], P(('ctx', 'exp')), may hold values from -0.09375 to 0.09375
- w_down: bfloat16 [128, 768, 4096], P(('ctx', 'exp')), may hold values from -0.21875 to 0.21875
Outputs:
- block_out: bfloat16 [2048, 4, 4096], P(('ctx', 'exp'))
Inputs may be any that keep to these rules, and one draw needn't show every extreme that they name: `expert_ids`: each token names 8 different experts; among the 64 tokens of one aligned block no expert is named more than 4 times.
All inputs are finite; a program needn't handle non-finite values.
Results may differ from a plain program's by a relative error of at most 0.025.
Values may be sent and summed in bfloat16 or wider, within the bound.
No kernel may reach another device: no remote copies, remote signals or barrier semaphores. Data moves between devices by JAX's collectives and lax.ppermute only.
A program may use at most 128 MiB of HBM per device.

v0:
```python
import math

import jax
import jax.numpy as jnp
from jax import lax
from jax.sharding import PartitionSpec as P

QUERY_HEAD_COUNT = 32
KEY_VALUE_HEADS = 2
HEAD_SIZE = 128
TOPK = 8


def local(
    queries,
    keys,
    values,
    residual,
    out_weight,
    norm_gain,
    expert_ids,
    expert_gates,
    w_gate,
    w_up,
    w_down,
):
    ctx_count = lax.axis_size("ctx")
    exp_count = lax.axis_size("exp")
    ctx_index = lax.axis_index("ctx")
    exp_index = lax.axis_index("exp")
    seq_count, local_len, features = queries.shape
    heads_here = features // HEAD_SIZE
    group_length = QUERY_HEAD_COUNT // KEY_VALUE_HEADS
    kv_offset = exp_index * heads_here // group_length * HEAD_SIZE
    key_mine = lax.dynamic_slice_in_dim(keys, kv_offset, HEAD_SIZE, 2)
    value_mine = lax.dynamic_slice_in_dim(values, kv_offset, HEAD_SIZE, 2)
    query_pos = ctx_index * local_len + jnp.arange(local_len, dtype=jnp.int32)
    query_heads = queries.reshape(seq_count, local_len, heads_here, HEAD_SIZE)
    scaling = HEAD_SIZE ** (-0.5)

    def absorb(running, key_part, value_part, key_pos):
        row_peak, denom_sum, weighted = running
        scores = (
            jnp.einsum("sqhd,skd->shqk", query_heads, key_part, preferred_element_type=jnp.float32)
            * scaling
        )
        visible = (key_pos[None, :] <= query_pos[:, None]) & (key_pos[None, :] >= 0)
        scores = jnp.where(visible[None, None], scores, -jnp.inf)
        new_peak = jnp.maximum(row_peak, jnp.max(scores, axis=3))
        shrink = jnp.exp(row_peak - new_peak)
        weights = jnp.exp(scores - new_peak[..., None])
        denom_sum = denom_sum * shrink + jnp.sum(weights, axis=3)
        contrib = jnp.einsum(
            "shqk,skd->qshd",
            weights.astype(jnp.bfloat16),
            value_part,
            preferred_element_type=jnp.float32,
        )
        weighted = weighted * jnp.transpose(shrink, (2, 0, 1))[..., None] + contrib
        return (new_peak, denom_sum, weighted)

    initial = (
        jnp.full((seq_count, heads_here, local_len), -1e30, jnp.float32),
        jnp.zeros((seq_count, heads_here, local_len), jnp.float32),
        jnp.zeros((local_len, seq_count, heads_here, HEAD_SIZE), jnp.float32),
    )
    key_part = lax.all_gather(key_mine, "ctx", axis=1, tiled=True)
    value_part = lax.all_gather(value_mine, "ctx", axis=1, tiled=True)
    key_count = key_part.shape[1]
    block_len = math.gcd(key_count, 512)

    def visit_block(block_no, current):
        first_key = block_no * block_len
        key_block = lax.dynamic_slice_in_dim(key_part, first_key, block_len, 1)
        value_block = lax.dynamic_slice_in_dim(value_part, first_key, block_len, 1)
        key_pos = first_key + jnp.arange(block_len, dtype=jnp.int32)
        needed = (key_pos[0] <= query_pos[-1]) & (key_pos[-1] >= 0)
        return lax.cond(
            needed,
            lambda stored: absorb(stored, key_block, value_block, key_pos),
            lambda stored: stored,
            current,
        )

    running = lax.fori_loop(0, key_count // block_len, visit_block, initial)
    row_peak, denom_sum, weighted = running
    attended = (weighted / jnp.transpose(denom_sum, (2, 0, 1))[..., None]).astype(jnp.bfloat16)
    attended = attended.reshape(local_len * seq_count, features)
    tok_here = residual.shape[0] * residual.shape[1]
    model_width = residual.shape[2]
    projected = lax.psum_scatter(
        jnp.dot(attended, out_weight, preferred_element_type=jnp.float32).astype(jnp.bfloat16),
        "exp",
        scatter_dimension=0,
        tiled=True,
    ).astype(jnp.float32)
    stream = (residual.reshape(tok_here, model_width).astype(jnp.float32) + projected).astype(
        jnp.bfloat16
    )
    stream_f = stream.astype(jnp.float32)
    mean_square = jnp.mean(stream_f * stream_f, axis=1, keepdims=True)
    normed = (stream_f * lax.rsqrt(mean_square + 1e-06) * norm_gain[None, :]).astype(jnp.bfloat16)
    experts_here = w_gate.shape[0]
    experts_all = experts_here * ctx_count * exp_count
    capacity = max(2, tok_here * TOPK * 9 // (8 * experts_all))
    flat_ids = expert_ids.reshape(-1)
    onehot = (flat_ids[:, None] == jnp.arange(experts_all, dtype=jnp.int32)[None, :]).astype(
        jnp.int32
    )
    before = jnp.cumsum(onehot, axis=0) - onehot
    slot_index = jnp.sum(before * onehot, axis=1)
    flat_slot = flat_ids * capacity + slot_index
    token_of = jnp.arange(tok_here * TOPK, dtype=jnp.int32) // TOPK
    outgoing = (
        jnp.zeros((experts_all * capacity, model_width), jnp.bfloat16)
        .at[flat_slot]
        .set(normed[token_of])
    )
    outgoing = outgoing.reshape(experts_all, capacity, model_width)
    arrived = lax.all_to_all(outgoing, ("ctx", "exp"), split_axis=0, concat_axis=0, tiled=True)
    source_count = arrived.shape[0] // experts_here
    slot_count = arrived.shape[1]
    grouped = arrived.reshape(source_count, experts_here, slot_count, model_width)
    gate_act = jnp.einsum("serd,edf->serf", grouped, w_gate, preferred_element_type=jnp.float32)
    up_act = jnp.einsum("serd,edf->serf", grouped, w_up, preferred_element_type=jnp.float32)
    expert_hidden = (jax.nn.silu(gate_act) * up_act).astype(jnp.bfloat16)
    produced = jnp.einsum(
        "serf,efd->serd", expert_hidden, w_down, preferred_element_type=jnp.float32
    )
    returned = lax.all_to_all(
        produced.astype(jnp.bfloat16).reshape(arrived.shape),
        ("ctx", "exp"),
        split_axis=0,
        concat_axis=0,
        tiled=True,
    )
    picked = returned.reshape(experts_all * capacity, model_width)[flat_slot].reshape(
        tok_here, TOPK, model_width
    )
    gate_rows = expert_gates.reshape(tok_here, TOPK)
    mixture = jnp.einsum(
        "tk,tkd->td", gate_rows, picked.astype(jnp.float32), preferred_element_type=jnp.float32
    )
    block_out = (stream_f + mixture).astype(jnp.bfloat16)
    return block_out.reshape(residual.shape)


def solution(mesh):
    in_specs = (
        P(None, "ctx", "exp"),
        P(None, "ctx", None),
        P(None, "ctx", None),
        P(("ctx", "exp"), None, None),
        P("exp", None),
        P(),
        P(("ctx", "exp"), None, None),
        P(("ctx", "exp"), None, None),
        P(("ctx", "exp"), None, None),
        P(("ctx", "exp"), None, None),
        P(("ctx", "exp"), None, None),
    )
    out_specs = P(("ctx", "exp"), None, None)
    return jax.shard_map(local, mesh=mesh, in_specs=in_specs, out_specs=out_specs, check_vma=False)
```

profile of v0, /device:TPU:1, one launch (start us, length us, event | category | flops | bytes accessed | tf_op | source)
XLA Modules:
  0.0 482.6 jit_solution(12501717434827200324)
XLA Ops:
  6.5 1.8 constant_dynamic-slice_fusion.1
  8.4 1.7 constant_dynamic-slice_fusion
  10.2 1.2 copy.26
  11.4 0.3 copy.27
  11.7 49.8 %all-gather.3.cloned.1.call-done = bf16[4,2048,128]{2,1,0:T(8,128)(2,1)} async-done(((bf16[4,256,128]{2,1,0:T(8,128)(2,1)}), bf16[4,2048,128]{2,1,0:T(8,128)(2,1)}) %all-gather.3.cloned.1.call-update) | async-done | bytes 2097168 | tf_op jit(solution)/shard_map/all_gather | solution.py:67
  61.5 53.1 %all-gather.5.cloned.1.call-done = bf16[4,2048,128]{2,1,0:T(8,128)(2,1)} async-done(((bf16[4,256,128]{2,1,0:T(8,128)(2,1)}), bf16[4,2048,128]{2,1,0:T(8,128)(2,1)}) %all-gather.5.cloned.1.call-update) | async-done | bytes 2097168 | tf_op jit(solution)/shard_map/all_gather | solution.py:68
  114.6 1.1 broadcast_in_dim.46
  115.7 19.3 %while.17 = (s32[]{:T(128)}, f32[4,2,256]{2,1,0:T(2,128)S(1)}, f32[4,2,256]{2,1,0:T(2,128)S(1)}, f32[256,4,2,128]{3,0,2,1:T(8,128)}, s32[256]{0:T(256)S(1)}, /*i...) while((s32[]{:T(128)}, f32[4,2,256]{2,1,0:T(2,128)S(1)}, ...), condition=%wide.region_5.6_spmd, body=%wide.region_0.5_spmd.sunk | while | flops 549198848 | bytes 25305488 | solution.py:85
  115.7 0.7 fusion.76
  116.3 0.7 slice.44
  119.0 5.8 %conditional.2 = ((f32[4,2,256]{2,1,0:T(2,128)S(1)}, f32[4,2,256]{2,1,0:T(2,128)S(1)}, f32[256,4,2,128]{3,0,2,1:T(8,128)})) conditional(s32[]{:T(128)} %bitcast.131, (f32[4,2,256]{2,1,0:T(2,128)S(1)}, f32[4,2,256]{2,1,0:T(2,128)S(1)}, f32[256,4,2,128]{3,0,2,1:T(8,128)}) %tuple.52, (s32[512]{0:T(512)S(1)}, s32[256]{0:T(256)S(1)}, s32[]{:T(128)}, ...), branch_computations={%region_1.1_spmd, %region_2.4_spmd} | conditional | flops 549198336 | bytes 25303170 | solution.py:78
  119.0 0.2 compare_and_fusion
  119.2 1.9 fusion.2
  121.1 2.6 fusion.12
  123.8 0.9 fusion.1
  124.8 0.7 fusion.76
  125.5 0.7 slice.44
  128.1 0.7 fusion.76
  128.8 0.7 slice.44
  131.5 0.7 fusion.76
  132.1 0.7 slice.44
  135.0 1.6 divide_convert_fusion
  136.5 0.5 copy.28
  137.1 5.6 %convolution_convert_fusion = bf16[1024,4096]{1,0:T(8,128)(2,1)} fusion(bf16[256,4096]{1,0:T(8,128)(2,1)S(1)} %copy-done, bf16[128,8,2,128]{3,2,1,0:T(2,128)(2,1)S(1)} %bitcast.133), kind=kOutput, calls=%fused_computation.30 | convolution fusion | flops 2151677952 | bytes 11010048 | tf_op jit(solution)/shard_map/dot_general | solution.py:92
  142.7 0.7 copy-done.6
  143.5 0.1 eq.29
  143.6 0.1 eq.25
  143.8 0.1 copy.32
  143.9 0.2 fusion.67
  144.3 0.1 mul.95
  144.5 0.2 fusion.66
  144.7 119.0 %reduce-scatter.2.cloned.1.call-done = bf16[64,4096]{1,0:T(8,128)(2,1)} async-done(((bf16[1024,4096]{1,0:T(8,128)(2,1)}), bf16[64,4096]{1,0:T(8,128)(2,1)}) %reduce-scatter.2.cloned.1.call-update) | async-done | bytes 524304 | tf_op jit(solution)/shard_map/reduce_scatter | solution.py:91
  263.8 1.3 fusion.54
  265.1 0.2 fusion.56
  265.3 21.2 %scatter_custom_fusion = bf16[512,4096]{1,0:T(8,128)(2,1)} fusion(s32[512]{0:T(512)S(1)} %bitcast.145, bf16[64,4096]{1,0:T(8,128)(2,1)S(1)} %fusion.56, s32[1024]{0:T(1024)S(1)} %pad_clamp_fusion.1, bf16[]{:T(256)} %constant.123.clone.1), kind=kCustom, calls=%fused_computation.40 | custom fusion | bytes 4194306 | tf_op jit(solution)/shard_map/scatter | solution.py:117
  286.5 7.2 %reshape.200 = bf16[128,4,4096]{2,1,0:T(4,128)(2,1)} reshape(bf16[512,4096]{1,0:T(8,128)(2,1)} %scatter_custom_fusion) | data formatting | bytes 8388608 | tf_op jit(solution)/shard_map/reshape | solution.py:119
  293.7 60.7 %all_to_all.10 = bf16[128,4,4096]{2,1,0:T(4,128)(2,1)S(1)} all-to-all(bf16[128,4,4096]{2,1,0:T(4,128)(2,1)} %reshape.200), channel_id=1, replica_groups=mesh['ctx'=8,'exp'=16] {'ctx','exp'}, dimensions={0} | all-to-all | bytes 8388608 | tf_op jit(solution)/shard_map/all_to_all | solution.py:120
  354.4 2.0 copy-done.2
  356.4 10.2 %fusion.29 = f32[128,4,768]{2,0,1:T(8,128)} fusion(bf16[1,4096,768]{2,1,0:T(8,128)(2,1)} %param.23, bf16[128,4,4096]{2,1,0:T(4,128)(2,1)S(1)} %all_to_all.10), kind=kOutput, calls=%fused_computation.35 | convolution fusion | flops 3221225472 | bytes 12058624 | tf_op jit(solution)/shard_map/serd,edf->serf/dot_general | solution.py:124
  366.6 19.8 %fusion.31 = bf16[128,4,4096]{2,0,1:T(8,128)(2,1)} fusion(bf16[1,768,4096]{2,1,0:T(8,128)(2,1)} %param.25, bf16[1,4096,768]{2,1,0:T(8,128)(2,1)} %param.24, bf16[128,4,4096]{2,1,0:T(4,128)(2,1)} %copy-done.2, f32[128,4,768]{2,0,1:T(8,128)} %fusion.29), kind=kOutput, calls=%fused_computation.37 | convolution fusion | flops 6446907392 | bytes 22544384 | tf_op jit(solution)/shard_map/serf,efd->serd/dot_general | solution.py:127
  386.4 7.6 %copy.36 = bf16[128,4,4096]{2,1,0:T(4,128)(2,1)} copy(bf16[128,4,4096]{2,0,1:T(8,128)(2,1)} %fusion.31) | data formatting | bytes 8388608 | tf_op jit(solution)/shard_map/convert_element_type | solution.py:131
  394.0 5.7 %all-to-all-start.1 = ((bf16[128,4,4096]{2,1,0:T(4,128)(2,1)}), bf16[128,4,4096]{2,1,0:T(4,128)(2,1)}, u32[]{:S(2)}, u32[]{:S(2)}) async-start(bf16[128,4,4096]{2,1,0:T(4,128)(2,1)} %copy.36), calls=%async_computation.2 | async-start | bytes 8388608 | tf_op jit(solution)/shard_map/all_to_all | solution.py:130
  399.8 52.5 %all-to-all-done.1 = bf16[128,4,4096]{2,1,0:T(4,128)(2,1)} async-done(((bf16[128,4,4096]{2,1,0:T(4,128)(2,1)}), bf16[128,4,4096]{2,1,0:T(4,128)(2,1)}, u32[]{:S(2)}, u32[]{:S(2)}) %all-to-all-start.1) | async-done | bytes 4194336 | tf_op jit(solution)/shard_map/all_to_all | solution.py:130
  452.3 6.9 %reshape.205 = bf16[512,4096]{1,0:T(8,128)(2,1)} reshape(bf16[128,4,4096]{2,1,0:T(4,128)(2,1)} %all-to-all-done.1) | data formatting | bytes 8388608 | tf_op jit(solution)/shard_map/reshape | solution.py:137
  459.3 11.3 %gather_fusion = bf16[512,4096]{1,0:T(8,128)(2,1)} fusion(bf16[512,4096]{1,0:T(8,128)(2,1)} %reshape.205, s32[1024]{0:T(1024)S(1)} %pad_clamp_fusion), kind=kCustom, calls=%fused_computation.1 | custom fusion | bytes 8390656 | tf_op jit(solution)/shard_map/gather | solution.py:137
  470.6 3.6 fusion.34
  474.1 0.7 fusion.57
  474.9 1.0 reshape.208
  (52 shorter events, 0.8 us)
Async XLA Ops:
  6.5 130.6 %copy-start = (bf16[256,4096]{1,0:T(8,128)(2,1)S(1)}, bf16[256,4096]{1,0:T(8,128)(2,1)}, u32[]{:S(2)}) copy-start(bf16[256,4096]{1,0:T(8,128)(2,1)} %param.19) | copy-start | bytes 6291460
  6.5 55.0 %all-gather.3.cloned.1.call-start = ((), (), s32[]{:S(2)}) async-start(), calls=%async_computation.3 | async-start | bytes 2359296 | tf_op jit(solution)/shard_map/all_gather | solution.py:67
  8.4 106.2 %all-gather.5.cloned.1.call-start = ((), (), s32[]{:S(2)}) async-start(), calls=%async_computation.4 | async-start | bytes 2359296 | tf_op jit(solution)/shard_map/all_gather | solution.py:68
  10.1 253.6 %reduce-scatter.2.cloned.1.call-start = ((), (), s32[]{:S(2)}) async-start(), calls=%async_computation.5 | async-start | bytes 8912896 | tf_op jit(solution)/shard_map/reduce_scatter | solution.py:91
  119.0 2.1 copy-start.3
  123.8 1.0 copy-start.4
  142.7 0.7 copy-start.6
  142.7 1.1 copy-start.5
  143.4 121.7 %copy-start.7 = (f32[4096]{0:T(1024)S(1)}, f32[4096]{0:T(1024)}, u32[]{:S(2)}) copy-start(f32[4096]{0:T(1024)} %param.20) | copy-start | bytes 49156
  354.4 2.0 copy-start.2
  394.0 5.8 %copy-start.8 = (f32[16,4,8]{0,2,1:T(8,128)S(1)}, f32[16,4,8]{0,2,1:T(8,128)}, u32[]{:S(2)}) copy-start(f32[16,4,8]{0,2,1:T(8,128)} %param.22) | copy-start | bytes 6148
  394.0 58.3 %all-to-all-start.1 = ((bf16[128,4,4096]{2,1,0:T(4,128)(2,1)}), bf16[128,4,4096]{2,1,0:T(4,128)(2,1)}, u32[]{:S(2)}, u32[]{:S(2)}) async-start(bf16[128,4,4096]{2,1,0:T(4,128)(2,1)} %copy.36), calls=%async_computation.2 | async-start | bytes 8388608 | tf_op jit(solution)/shard_map/all_to_all | solution.py:130
  470.6 5.3 %copy-start.1 = (bf16[256,4096]{1,0:T(8,128)(2,1)S(1)}, bf16[256,4096]{1,0:T(8,128)(2,1)}, u32[]{:S(2)}) copy-start(bf16[256,4096]{1,0:T(8,128)(2,1)} %param.19) | copy-start | bytes 6291460
Sparse Core Ops, SparseCore 0:
  9.0 52.4 all-gather.2
  63.1 51.4 all-gather.4
  142.8 120.8 reduce-scatter.1
where the time goes:
time: 487 us; the launch traced here: 483 us
  waiting for transfers between devices  274 us (56%)
  local copies, waits for them, and re-layouts  70.8 us (15%)
  blocking collectives  60.7 us (12%)
  matrix products  43.6 us (9%)
  between operations  13.5 us (3%)
  loops' own time  8.26 us (2%)
  starting transfers between devices  5.83 us (1%)
  other arithmetic  5.42 us (1%)
    reduce_scatter x1, waiting for transfers between devices, local(): lax.psum_scatter(jnp.dot(attended, out_weight, preferred_element_type=jnp...  119 us
    all_to_all x1, blocking collectives, local(): lax.all_to_all(outgoing, ('ctx', 'exp'), split_axis=0, concat_axis=0, til...  60.7 us
    all_gather x1, waiting for transfers between devices, local(): value_part = lax.all_gather(value_mine, 'ctx', axis=1, tiled=True)  53.1 us
    all_to_all x1, waiting for transfers between devices, local(): lax.all_to_all(produced.astype(jnp.bfloat16).reshape(arrived.shape), ('ct...  52.5 us
    all_gather x1, waiting for transfers between devices, local(): key_part = lax.all_gather(key_mine, 'ctx', axis=1, tiled=True)  49.8 us
    scatter x1, local copies, waits for them, and re-layouts, local(): outgoing = jnp.zeros((experts_all * capacity, model_width), jnp.bfloat16)...  21.2 us
    dot_general x1, matrix products, local(): jnp.einsum('serf,efd->serd', expert_hidden, w_down, preferred_element_typ...  19.8 us
    gather x1, local copies, waits for them, and re-layouts, local(): returned.reshape(experts_all * capacity, model_width)[flat_slot]  11.3 us
  transfers between devices with their start and end apart: 4, of which 4 were waited for; matrix products, arithmetic and copies ran while one was open for 1% of the time, Pallas kernels for 0%

commit v1 on v0

v1 whole, which is shorter than its diff:
```python
import jax
import jax.numpy as jnp
from jax import lax
from jax.experimental import pallas as pl
from jax.experimental.pallas import tpu as pltpu
from jax.sharding import Mesh
from jax.sharding import PartitionSpec as P

HEAD = 128
TOPK = 8
CTX = ("x", "zl")
EXP = ("zh", "y", "core")
ALL = CTX + EXP
QUAD = ("zh", "core")
SHAPE = (4, 2, 2, 4, 2)
LOG2E = 1.4426950408889634
F32 = jnp.float32
BF16 = jnp.bfloat16
NEG = -1e30
VMEM = 48 * 1024 * 1024


def nt(a, b):
    return lax.dot_general(a, b, (((1,), (1,)), ((), ())), preferred_element_type=F32)


def tn(a, b):
    return lax.dot_general(a, b, (((0,), (0,)), ((), ())), preferred_element_type=F32)


def attention_kernel(ctx_ref, q_ref, kv_ref, out_ref, top_ref, sum_ref, acc_ref):
    ctx = ctx_ref[0]
    length = q_ref.shape[1]
    rows = 2 * length
    factor = HEAD**-0.5 * LOG2E
    top_ref[...] = jnp.full_like(top_ref, NEG)
    sum_ref[...] = jnp.zeros_like(sum_ref)
    acc_ref[...] = jnp.zeros_like(acc_ref)

    def block(index, masked):
        kv = kv_ref[index]
        for c in range(4):
            g = c // 2
            key = kv[:, g * HEAD : (g + 1) * HEAD]
            value = kv[:, (2 + g) * HEAD : (3 + g) * HEAD]
            query = jnp.concatenate([q_ref[c, :, :HEAD], q_ref[c, :, HEAD:]], axis=0)
            scores = nt(key, query)
            if masked:
                key_pos = lax.broadcasted_iota(jnp.int32, (length, rows), 0)
                query_pos = lax.broadcasted_iota(jnp.int32, (length, rows), 1) % length
                scores = jnp.where(key_pos <= query_pos, scores, NEG)
            old = top_ref[c]
            new = jnp.maximum(old, jnp.max(scores, axis=0, keepdims=True))
            shrink = jnp.exp2((old - new) * factor)
            weights = jnp.exp2((scores - new) * factor)
            sum_ref[c] = sum_ref[c] * shrink + jnp.sum(weights, axis=0, keepdims=True)
            acc_ref[c] = acc_ref[c] * shrink + tn(value, weights.astype(BF16))
            top_ref[c] = new

    block(ctx, True)

    @pl.loop(0, ctx)
    def _(index):
        block(index, False)

    for c in range(4):
        done = (acc_ref[c] / sum_ref[c]).T.astype(BF16)
        out_ref[:, 256 * c : 256 * c + HEAD] = done[:length]
        out_ref[:, 256 * c + HEAD : 256 * (c + 1)] = done[length:]


def attention(ctx, q4, kv):
    length = q4.shape[1]
    return pl.pallas_call(
        attention_kernel,
        out_shape=jax.ShapeDtypeStruct((length, 1024), BF16),
        in_specs=[
            pl.BlockSpec(memory_space=pltpu.SMEM),
            pl.BlockSpec(memory_space=pltpu.VMEM),
            pl.BlockSpec(memory_space=pltpu.VMEM),
        ],
        out_specs=pl.BlockSpec(memory_space=pltpu.VMEM),
        scratch_shapes=[
            pltpu.VMEM((4, 1, 2 * length), F32),
            pltpu.VMEM((4, 1, 2 * length), F32),
            pltpu.VMEM((4, HEAD, 2 * length), F32),
        ],
        compiler_params=pltpu.CompilerParams(vmem_limit_bytes=VMEM),
        name="attention",
    )(ctx, q4, kv)


def project_kernel(att_ref, w0_ref, w1_ref, w2_ref, w3_ref, out_ref):
    total = None
    for c, w_ref in enumerate((w0_ref, w1_ref, w2_ref, w3_ref)):
        part = jnp.dot(
            att_ref[:, 256 * c : 256 * (c + 1)], w_ref[...], preferred_element_type=F32
        )
        total = part if total is None else total + part
    out_ref[...] = total.astype(BF16)


def project(att, weights):
    rows, width = att.shape[0], weights[0].shape[1]
    tile = 1024
    return pl.pallas_call(
        project_kernel,
        grid=(width // tile,),
        out_shape=jax.ShapeDtypeStruct((rows, width), BF16),
        in_specs=[pl.BlockSpec((rows, 1024), lambda i: (0, 0))]
        + [pl.BlockSpec((256, tile), lambda i: (0, i))] * 4,
        out_specs=pl.BlockSpec((rows, tile), lambda i: (0, i)),
        compiler_params=pltpu.CompilerParams(vmem_limit_bytes=VMEM),
        name="project",
    )(att, *weights)


STEPS = 4


def pick(rows, half):
    r = lax.broadcasted_iota(jnp.int32, (rows, 2 * rows), 0)
    c = lax.broadcasted_iota(jnp.int32, (rows, 2 * rows), 1)
    return jnp.where(c == (r // 4) * 8 + 4 * half + r % 4, 1.0, 0.0).astype(BF16)


def expert_kernel(r_ref, wg_ref, wu_ref, wda_ref, wdb_ref, out_ref, gate_ref, up_ref, hid_ref):
    step = pl.program_id(0)
    total = hid_ref.shape[0]
    part = 128

    @pl.when(step == 0)
    def _():
        gate_ref[...] = jnp.zeros_like(gate_ref)
        up_ref[...] = jnp.zeros_like(up_ref)

    @pl.when(step < STEPS)
    def _():
        for half in range(2):
            matrix = pick(part, half)
            x = jnp.concatenate(
                [
                    jnp.dot(
                        matrix,
                        r_ref[2 * part * b : 2 * part * (b + 1), :],
                        preferred_element_type=F32,
                    ).astype(BF16)
                    for b in range(total // part)
                ],
                axis=0,
            )
            gate_ref[...] += jnp.dot(x, wg_ref[half], preferred_element_type=F32)
            up_ref[...] += jnp.dot(x, wu_ref[half], preferred_element_type=F32)

    @pl.when(step == STEPS - 1)
    def _():
        gate = gate_ref[...]
        hid_ref[...] = (gate / (1.0 + jnp.exp(-gate)) * up_ref[...]).astype(BF16)

    @pl.when(step >= STEPS)
    def _():
        hidden = hid_ref[...]
        low = jnp.dot(hidden, wda_ref[...], preferred_element_type=F32).astype(BF16)
        high = jnp.dot(hidden, wdb_ref[...], preferred_element_type=F32).astype(BF16)
        for b in range(total // part):
            rows = slice(part * b, part * (b + 1))
            out_ref[2 * part * b : 2 * part * (b + 1), :] = (
                tn(pick(part, 0), low[rows]) + tn(pick(part, 1), high[rows])
            ).astype(BF16)


def experts(arrived, w_gate, w_up, w_down):
    rows, width = arrived.shape
    hidden = w_down.shape[0]
    tile = width // STEPS
    last = STEPS - 1
    w_in = pl.BlockSpec((2, tile, hidden), lambda i: (0, jnp.minimum(i, last), 0))
    return pl.pallas_call(
        expert_kernel,
        grid=(2 * STEPS,),
        out_shape=jax.ShapeDtypeStruct((rows, width), BF16),
        in_specs=[
            pl.BlockSpec((rows, tile), lambda i: (0, jnp.minimum(i, last))),
            w_in,
            w_in,
            pl.BlockSpec((hidden, tile), lambda i: (0, jnp.maximum(i - STEPS, 0))),
            pl.BlockSpec((hidden, tile), lambda i: (0, jnp.maximum(i - STEPS, 0) + STEPS)),
        ],
        out_specs=pl.BlockSpec((rows, tile), lambda i: (0, jnp.maximum(i - STEPS, 0))),
        scratch_shapes=[
            pltpu.VMEM((rows // 2, hidden), F32),
            pltpu.VMEM((rows // 2, hidden), F32),
            pltpu.VMEM((rows // 2, hidden), BF16),
        ],
        compiler_params=pltpu.CompilerParams(vmem_limit_bytes=VMEM),
        name="experts",
    )(
        arrived,
        w_gate.reshape(2, width, hidden),
        w_up.reshape(2, width, hidden),
        w_down,
        w_down,
    )


def routing(expert_ids, expert_gates, experts_all, capacity):
    positions, sequences, _ = expert_ids.shape
    tokens = positions * sequences
    flat_ids = expert_ids.reshape(-1)
    onehot = (flat_ids[:, None] == jnp.arange(experts_all, dtype=jnp.int32)[None, :]).astype(
        jnp.int32
    )
    before = jnp.cumsum(onehot, axis=0) - onehot
    slot = jnp.sum(before * onehot, axis=1)
    place = (flat_ids * 2 * capacity + slot).reshape(tokens, TOPK)
    rows = jnp.arange(2 * capacity * experts_all, dtype=jnp.int32)
    place_sp = place.reshape(positions, sequences, TOPK).transpose(1, 0, 2).reshape(tokens, TOPK)

    def dispatch_half(half):
        hit = rows[:, None, None] == place_sp[None] + half * capacity
        return jnp.any(hit, axis=2)

    dispatch = jnp.concatenate([dispatch_half(0), dispatch_half(1)], axis=1).astype(BF16)
    gates = expert_gates.reshape(tokens, TOPK)

    def combine_half(half):
        hit = rows[None, None, :] == (place + half * capacity)[:, :, None]
        return jnp.sum(jnp.where(hit, gates[:, :, None], 0.0), axis=1)

    combine = jnp.concatenate([combine_half(0), combine_half(1)], axis=0)
    high = combine.astype(BF16)
    low = (combine - high.astype(F32)).astype(BF16)
    return dispatch, jnp.concatenate([high, low], axis=0)


def local(
    queries,
    keys,
    values,
    residual,
    out_weight,
    norm_gain,
    expert_ids,
    expert_gates,
    w_gate,
    w_up,
    w_down,
):
    ctx_index = lax.axis_index(CTX)
    zh = lax.axis_index("zh")
    quad = lax.axis_index(QUAD)
    quad_count = lax.axis_size(QUAD)
    ctx_count = lax.axis_size(CTX)
    exp_count = lax.axis_size(EXP)
    sequences, length, _ = queries.shape
    width = residual.shape[2]

    key_seq = lax.dynamic_index_in_dim(keys, quad, 0, False)
    value_seq = lax.dynamic_index_in_dim(values, quad, 0, False)

    def ordered(a):
        return jnp.where(zh == 0, a, jnp.concatenate([a[:, HEAD:], a[:, :HEAD]], axis=1))

    kv_mine = jnp.concatenate([ordered(key_seq), ordered(value_seq)], axis=1)
    kv_send = jnp.broadcast_to(kv_mine[None], (ctx_count,) + kv_mine.shape)

    chunks = []
    for s in range(quad_count):
        part = lax.dynamic_index_in_dim(queries, quad ^ s, 0, False)
        if s:
            part = lax.ppermute(part, QUAD, [(i, i ^ s) for i in range(quad_count)])
        chunks.append(part)

    swap = [(0, 1), (1, 0)]
    across = []
    for i in range(4):
        zl, zh_i = i // 2, i % 2
        across.append((i, (1 - zl) * 2 + (1 - zh_i)))
    w_core = lax.ppermute(out_weight, "core", swap)
    w_other = lax.ppermute(out_weight, ("zl", "zh"), across)
    w_both = lax.ppermute(w_other, "core", swap)

    kv = lax.all_to_all(kv_send, CTX, 0, 0, tiled=True)
    attended = attention(ctx_index[None].astype(jnp.int32), jnp.stack(chunks), kv)
    partial_sums = project(attended, (out_weight, w_core, w_other, w_both))
    parts = lax.all_to_all(
        partial_sums.reshape(exp_count, length // exp_count, width), EXP, 0, 0, tiled=True
    )
    positions = length // exp_count
    parts = parts.reshape(2, exp_count // 4, 2, positions, width)
    projected = jnp.sum(parts.astype(F32), axis=1)
    tokens = sequences * positions
    stream = (
        residual.astype(F32).transpose(1, 0, 2) + projected.reshape(sequences, positions, width)
    ).astype(BF16)
    stream = stream.reshape(tokens, width)
    stream_f = stream.astype(F32)
    mean_square = jnp.mean(stream_f * stream_f, axis=1, keepdims=True)
    normed = (stream_f * lax.rsqrt(mean_square + 1e-06) * norm_gain[None, :]).astype(BF16)

    experts_all = w_gate.shape[0] * ctx_count * exp_count
    capacity = tokens * TOPK // experts_all
    dispatch, combine = routing(expert_ids, expert_gates, experts_all, capacity)
    half = width // 2
    halves = jnp.concatenate([normed[:, :half], normed[:, half:]], axis=0)
    outgoing = jnp.dot(dispatch, halves, preferred_element_type=F32).astype(BF16)
    arrived = lax.all_to_all(
        outgoing.reshape(experts_all, 2 * capacity, half), ALL, 0, 0, tiled=True
    )
    produced = experts(
        arrived.reshape(experts_all * 2 * capacity, half), w_gate[0], w_up[0], w_down[0]
    )
    returned = lax.all_to_all(
        produced.reshape(experts_all, 2 * capacity, half), ALL, 0, 0, tiled=True
    )
    mixture = jnp.dot(
        combine, returned.reshape(experts_all * 2 * capacity, half), preferred_element_type=F32
    )
    mixture = mixture[: 2 * tokens] + mixture[2 * tokens :]
    mixture = jnp.concatenate([mixture[:tokens], mixture[tokens:]], axis=1)
    back = stream_f.reshape(sequences, positions, width).transpose(1, 0, 2)
    return (back + mixture.reshape(positions, sequences, width)).astype(BF16)


def solution(mesh):
    fine = Mesh(mesh.devices.reshape(SHAPE), ALL)
    rows = P(ALL, None, None)
    in_specs = (
        P(None, CTX, EXP),
        P(None, CTX, None),
        P(None, CTX, None),
        rows,
        P(EXP, None),
        P(),
        rows,
        rows,
        rows,
        rows,
        rows,
    )
    return jax.shard_map(local, mesh=fine, in_specs=in_specs, out_specs=rows, check_vma=False)
```

time: 487 us -> 290 us (0.60)
  waiting for transfers between devices: 274 us -> 149 us
  local copies, waits for them, and re-layouts: 70.8 us -> 7.69 us
  matrix products: 43.6 us -> 4.74 us
  Pallas kernels: 0 us -> 26.6 us
  starting transfers between devices: 5.83 us -> 28.2 us
  between operations: 13.5 us -> 0.34 us
  loops' own time: 8.26 us -> 0 us
  blocking collectives: 60.7 us -> 68.3 us
    reduce_scatter x1 -> x0, waiting for transfers between devices: 119 us -> none  [local(): lax.psum_scatter(jnp.dot(attended, out_weight, preferred_element_type=jnp...]
    all_gather x2 -> x0, waiting for transfers between devices: 103 us -> none  [the longest x1 53.1 us: local(): value_part = lax.all_gather(value_mine, 'ctx', axis=1, tiled=True)]
    ppermute x0 -> x6, waiting for transfers between devices: none -> 72.3 us  [the longest x1 43.6 us: local(): w_other = lax.ppermute(out_weight, ('zl', 'zh'), across)]
    dot_general x6 -> x2, matrix products: 43.6 us -> 4.74 us  [the longest x1 3.43 us: local(): jnp.dot(combine, returned.reshape(experts_all * 2 * capacity, half), pref...]
    pallas_call x0 -> x3, Pallas kernels: none -> 26.6 us  [the longest x1 18.7 us: experts(): pl.pallas_call(expert_kernel, grid=(2 * STEPS,), out_shape=jax.ShapeDtype...]
    all_to_all x1 -> x3, waiting for transfers between devices: 52.5 us -> 76.2 us  [the longest x1 50.4 us: local(): lax.all_to_all(produced.reshape(experts_all, 2 * capacity, half), ALL, 0,...]
    scatter x1 -> x0, local copies, waits for them, and re-layouts: 21.2 us -> none  [local(): outgoing = jnp.zeros((experts_all * capacity, model_width), jnp.bfloat16)...]
    reshape x3 -> x1, local copies, waits for them, and re-layouts: 15.2 us -> 0.31 us  [local(): return (back + mixture.reshape(positions, sequences, width)).astype(BF16)]
  transfers between devices with their start and end apart: 4 -> 9, of which waited for: 4 -> 5; matrix products, arithmetic and copies ran while one was open for 1% -> 3% of each run, Pallas kernels for 0% -> 1%
where the time goes in v1:
time: 290 us
  waiting for transfers between devices  149 us (51%)
  blocking collectives  68.3 us (24%)
  starting transfers between devices  28.2 us (10%)
  Pallas kernels  26.6 us (9%)
  local copies, waits for them, and re-layouts  7.69 us (3%)
  other arithmetic  5.56 us (2%)
  matrix products  4.74 us (2%)
    all_to_all x1, blocking collectives, local(): lax.all_to_all(outgoing.reshape(experts_all, 2 * capacity, half), ALL, 0,...  68.3 us
    all_to_all x1, waiting for transfers between devices, local(): lax.all_to_all(produced.reshape(experts_all, 2 * capacity, half), ALL, 0,...  50.4 us
    ppermute x1, waiting for transfers between devices, local(): w_other = lax.ppermute(out_weight, ('zl', 'zh'), across)  43.6 us
    ppermute x3, waiting for transfers between devices, local(): part = lax.ppermute(part, QUAD, [(i, i ^ s) for i in range(quad_count)])  28.7 us
    all_to_all x1, waiting for transfers between devices, local(): lax.all_to_all(partial_sums.reshape(exp_count, length // exp_count, width...  25.8 us
    pallas_call x1, Pallas kernels, experts(): pl.pallas_call(expert_kernel, grid=(2 * STEPS,), out_shape=jax.ShapeDtype...  18.7 us
    all_to_all x1, starting transfers between devices, local(): lax.all_to_all(partial_sums.reshape(exp_count, length // exp_count, width...  7.41 us
    pallas_call x1, Pallas kernels, project(): pl.pallas_call(project_kernel, grid=(width // tile,), out_shape=jax.Shape...  6.18 us
  transfers between devices with their start and end apart: 9, of which 5 were waited for; matrix products, arithmetic and copies ran while one was open for 3% of the time, Pallas kernels for 1%

profile of v1, /device:TPU:1, one launch (start us, length us, event | category | flops | bytes accessed | tf_op | source)
XLA Modules:
  0.0 289.9 jit_solution(3031180465737254758)
XLA Ops:
  0.0 4.6 %collective-permute-start.4 = (bf16[256,4096]{1,0:T(8,128)(2,1)}, bf16[256,4096]{1,0:T(8,128)(2,1)}, u32[]{:S(2)}, u32[]{:S(2)}) collective-permute-start(bf16[256,4096]{1,0:T(8,128)(2,1)} %w0_ref.1), channel_id=1, source_target_pairs={{0,24},{8,16},{16,8},{24,0},{1,25},{9,17},{17,9},{25,1},{2,26},{10... | collective-permute-start | bytes 6291464 | tf_op jit(solution)/shard_map/ppermute | solution.py:280
  4.6 1.0 collective-permute-start.3
  5.5 1.0 dynamic-slice_bitcast_fusion
  6.6 43.6 %collective-permute-done.4.w2_ref = bf16[256,4096]{1,0:T(8,128)(2,1)} collective-permute-done((bf16[256,4096]{1,0:T(8,128)(2,1)}, bf16[256,4096]{1,0:T(8,128)(2,1)}, u32[]{:S(2)}, u32[]{:S(2)}) %collective-permute-start.4) | collective-permute-done | bytes 2097184 | tf_op jit(solution)/shard_map/ppermute | solution.py:280
  50.3 1.2 collective-permute-start.5
  51.5 1.5 broadcast_in_dim.36
  53.1 4.2 %all-to-all-start = ((bf16[8,256,512]{2,1,0:T(8,128)(2,1)}), bf16[8,256,512]{2,1,0:T(8,128)(2,1)S(1)}, u32[]{:S(2)}, u32[]{:S(2)}) async-start(bf16[8,256,512]{2,1,0:T(8,128)(2,1)} %broadcast_in_dim.36), calls=%async_computation | async-start | bytes 4194304 | tf_op jit(solution)/shard_map/all_to_all | solution.py:283
  57.3 0.4 collective-permute-start
  57.7 3.6 %collective-permute-start.1 = (bf16[256,256]{1,0:T(8,128)(2,1)S(1)}, bf16[256,256]{1,0:T(8,128)(2,1)S(1)}, u32[]{:S(2)}, u32[]{:S(2)}) collective-permute-start(bf16[256,256]{1,0:T(8,128)(2,1)S(1)} %get-tuple-element.16), channel_id=1, source_target_pairs={{0,8},{1,9},{8,0},{9,1},{2,10},{3,11},{10,2},{11,3},{4,12},{5,13},... | collective-permute-start | bytes 393224 | tf_op jit(solution)/shard_map/ppermute | solution.py:271
  61.2 0.1 collective-permute-start.2
  61.4 25.3 %collective-permute-done.1 = bf16[256,256]{1,0:T(8,128)(2,1)S(1)} collective-permute-done((bf16[256,256]{1,0:T(8,128)(2,1)S(1)}, bf16[256,256]{1,0:T(8,128)(2,1)S(1)}, u32[]{:S(2)}, u32[]{:S(2)}) %collective-permute-start.1) | collective-permute-done | bytes 131104 | tf_op jit(solution)/shard_map/ppermute | solution.py:271
  86.7 3.4 %collective-permute-done.2 = bf16[256,256]{1,0:T(8,128)(2,1)S(1)} collective-permute-done((bf16[256,256]{1,0:T(8,128)(2,1)S(1)}, bf16[256,256]{1,0:T(8,128)(2,1)S(1)}, u32[]{:S(2)}, u32[]{:S(2)}) %collective-permute-start.2) | collective-permute-done | bytes 131104 | tf_op jit(solution)/shard_map/ppermute | solution.py:271
  90.1 1.7 attention.1.att_ref
  91.9 6.2 %project.1 = bf16[256,4096]{1,0:T(8,128)(2,1)} custom-call(bf16[256,1024]{1,0:T(8,128)(2,1)S(1)} %attention.1.att_ref, bf16[256,4096]{1,0:T(8,128)(2,1)S(1)} %copy-done.1, bf16[256,4096]{1,0:T(8,128)(2,1)} %collective-permute-done.3.w1_ref, bf16[256,4096]{1,0:T(8,128)(2,1)} %collective-permute-done.4.w2_ref, bf16[256,4096]{1,0:T(8,128)(2,1)} %collective-permute-done.5.w3_ref), custom_call_target="tpu_custom_call" | custom-call | tf_op jit(solution)/shard_map/project/pallas_call | solution.py:106
  98.1 7.4 %all-to-all-start.1 = ((bf16[16,16,4096]{2,1,0:T(8,128)(2,1)}), bf16[16,16,4096]{2,1,0:T(8,128)(2,1)S(1)}, u32[]{:S(2)}, u32[]{:S(2)}) async-start(bf16[16,16,4096]{2,1,0:T(8,128)(2,1)} %bitcast.10), calls=%async_computation.1 | async-start | bytes 4194304 | tf_op jit(solution)/shard_map/all_to_all | solution.py:286
  105.6 0.1 eq.89
  105.7 0.1 eq.85
  105.8 0.1 copy.40
  105.9 0.2 fusion.20
  106.2 0.2 fusion.19
  106.5 0.1 reduce_sum.54
  106.6 0.1 copy.47
  106.7 0.1 eq.99
  106.8 0.1 copy.48
  106.9 0.1 copy.49
  106.9 1.3 fusion.2
  108.3 25.8 %all-to-all-done.1 = bf16[16,16,4096]{2,1,0:T(8,128)(2,1)S(1)} async-done(((bf16[16,16,4096]{2,1,0:T(8,128)(2,1)}), bf16[16,16,4096]{2,1,0:T(8,128)(2,1)S(1)}, u32[]{:S(2)}, u32[]{:S(2)}) %all-to-all-start.1) | async-done | bytes 2097184 | tf_op jit(solution)/shard_map/all_to_all | solution.py:286
  134.1 0.3 convert_reduce_fusion
  134.4 0.4 fusion.7
  134.8 0.2 multiply_reduce_fusion
  135.0 0.1 rsqrt.12
  135.1 0.2 fusion.5
  135.4 1.3 convert_bitcast_fusion
  136.7 68.3 %all_to_all.20 = bf16[128,8,2048]{2,1,0:T(8,128)(2,1)} all-to-all(bf16[128,8,2048]{2,1,0:T(8,128)(2,1)S(1)} %convert_bitcast_fusion), channel_id=1, replica_groups=mesh['x'=4,'zl'=2,'zh'=2,'y'=4,'core'=2] {'x','zl','zh','y','core'}, dimensions={0} | all-to-all | bytes 8388608 | tf_op jit(solution)/shard_map/all_to_all | solution.py:307
  204.9 18.7 %experts.1 = bf16[1024,2048]{1,0:T(8,128)(2,1)S(1)} custom-call(bf16[1024,2048]{1,0:T(8,128)(2,1)} %bitcast.65, bf16[2,2048,768]{2,1,0:T(8,128)(2,1)} %bitcast.67, bf16[2,2048,768]{2,1,0:T(8,128)(2,1)} %bitcast.68, bf16[768,4096]{1,0:T(8,128)(2,1)} %bitcast.63, bf16[768,4096]{1,0:T(8,128)(2,1)} %bitcast.64), custom_call_target="tpu_custom_call" | custom-call | tf_op jit(solution)/shard_map/experts/pallas_call | solution.py:178
  223.7 2.0 copy-done
  225.6 5.7 %all-to-all-start.3 = ((bf16[128,8,2048]{2,1,0:T(8,128)(2,1)}), bf16[128,8,2048]{2,1,0:T(8,128)(2,1)}, u32[]{:S(2)}, u32[]{:S(2)}) async-start(bf16[128,8,2048]{2,1,0:T(8,128)(2,1)} %bitcast.62), calls=%async_computation.3 | async-start | bytes 8388608 | tf_op jit(solution)/shard_map/all_to_all | solution.py:313
  231.4 0.1 reduce_sum.51
  231.6 0.1 copy.44
  231.7 0.1 copy.46
  231.9 1.6 select_reduce_fusion.1
  233.6 50.4 %all-to-all-done.3 = bf16[128,8,2048]{2,1,0:T(8,128)(2,1)} async-done(((bf16[128,8,2048]{2,1,0:T(8,128)(2,1)}), bf16[128,8,2048]{2,1,0:T(8,128)(2,1)}, u32[]{:S(2)}, u32[]{:S(2)}) %all-to-all-start.3) | async-done | bytes 4194336 | tf_op jit(solution)/shard_map/all_to_all | solution.py:313
  284.0 3.4 %fusion = f32[256,2048]{1,0:T(8,128)S(1)} fusion(bf16[128,8,2048]{2,1,0:T(8,128)(2,1)} %all-to-all-done.3, bf16[128,1024]{1,0:T(8,128)(2,1)S(1)} %subtract_convert_fusion, bf16[128,1024]{1,0:T(8,128)(2,1)S(1)} %fusion.17), kind=kOutput, calls=%fused_computation.1 | convolution fusion | flops 1074790400 | bytes 6815744 | tf_op jit(solution)/shard_map/dot_general | solution.py:316
  287.4 0.1 slice_add_fusion
  287.6 0.1 fusion.26
  287.7 0.3 reshape.104
  288.0 0.6 fusion.6
  288.7 1.2 copy.51
  (42 shorter events, 0.9 us)
Async XLA Ops:
  0.0 50.3 %collective-permute-start.4 = (bf16[256,4096]{1,0:T(8,128)(2,1)}, bf16[256,4096]{1,0:T(8,128)(2,1)}, u32[]{:S(2)}, u32[]{:S(2)}) collective-permute-start(bf16[256,4096]{1,0:T(8,128)(2,1)} %w0_ref.1), channel_id=1, source_target_pairs={{0,24},{8,16},{16,8},{24,0},{1,25},{9,17},{17,9},{25,1},{2,26},{10... | collective-permute-start | bytes 6291464 | tf_op jit(solution)/shard_map/ppermute | solution.py:280
  4.6 87.3 %collective-permute-start.3 = (bf16[256,4096]{1,0:T(8,128)(2,1)}, bf16[256,4096]{1,0:T(8,128)(2,1)}, u32[]{:S(2)}, u32[]{:S(2)}) collective-permute-start(bf16[256,4096]{1,0:T(8,128)(2,1)} %w0_ref.1), channel_id=1, source_target_pairs={{0,1},{1,0},{2,3},{3,2},{4,5},{5,4},{6,7},{7,6},{8,9},{9,8},{10,11... | collective-permute-start | bytes 6291464 | tf_op jit(solution)/shard_map/ppermute | solution.py:279
  50.3 41.6 %collective-permute-start.5 = (bf16[256,4096]{1,0:T(8,128)(2,1)}, bf16[256,4096]{1,0:T(8,128)(2,1)}, u32[]{:S(2)}, u32[]{:S(2)}) collective-permute-start(bf16[256,4096]{1,0:T(8,128)(2,1)} %collective-permute-done.4.w2_ref), channel_id=1, source_target_pairs={{0,1},{1,0},{2,3},{3,2},{4,5},{5,4},{6,7},{7,6},{8,9},{9,8},{10,11... | collective-permute-start | bytes 6291464 | tf_op jit(solution)/shard_map/ppermute | solution.py:281
  53.1 4.2 %copy-start.2 = (bf16[4,256,256]{2,1,0:T(8,128)(2,1)S(1)}, bf16[4,256,256]{2,1,0:T(8,128)(2,1)}, u32[]{:S(2)}) copy-start(bf16[4,256,256]{2,1,0:T(8,128)(2,1)} %param.11) | copy-start | bytes 1572868
  53.1 37.0 %all-to-all-start = ((bf16[8,256,512]{2,1,0:T(8,128)(2,1)}), bf16[8,256,512]{2,1,0:T(8,128)(2,1)S(1)}, u32[]{:S(2)}, u32[]{:S(2)}) async-start(bf16[8,256,512]{2,1,0:T(8,128)(2,1)} %broadcast_in_dim.36), calls=%async_computation | async-start | bytes 4194304 | tf_op jit(solution)/shard_map/all_to_all | solution.py:283
  57.3 4.1 %collective-permute-start = (bf16[256,256]{1,0:T(8,128)(2,1)S(1)}, bf16[256,256]{1,0:T(8,128)(2,1)S(1)}, u32[]{:S(2)}, u32[]{:S(2)}) collective-permute-start(bf16[256,256]{1,0:T(8,128)(2,1)S(1)} %get-tuple-element.14), channel_id=1, source_target_pairs={{0,1},{1,0},{8,9},{9,8},{2,3},{3,2},{10,11},{11,10},{4,5},{5,4},{1... | collective-permute-start | bytes 393224 | tf_op jit(solution)/shard_map/ppermute | solution.py:271
  57.7 29.0 %collective-permute-start.1 = (bf16[256,256]{1,0:T(8,128)(2,1)S(1)}, bf16[256,256]{1,0:T(8,128)(2,1)S(1)}, u32[]{:S(2)}, u32[]{:S(2)}) collective-permute-start(bf16[256,256]{1,0:T(8,128)(2,1)S(1)} %get-tuple-element.16), channel_id=1, source_target_pairs={{0,8},{1,9},{8,0},{9,1},{2,10},{3,11},{10,2},{11,3},{4,12},{5,13},... | collective-permute-start | bytes 393224 | tf_op jit(solution)/shard_map/ppermute | solution.py:271
  61.2 28.8 %collective-permute-start.2 = (bf16[256,256]{1,0:T(8,128)(2,1)S(1)}, bf16[256,256]{1,0:T(8,128)(2,1)S(1)}, u32[]{:S(2)}, u32[]{:S(2)}) collective-permute-start(bf16[256,256]{1,0:T(8,128)(2,1)S(1)} %get-tuple-element.15), channel_id=1, source_target_pairs={{0,9},{1,8},{8,1},{9,0},{2,11},{3,10},{10,3},{11,2},{4,13},{5,12},... | collective-permute-start | bytes 393224 | tf_op jit(solution)/shard_map/ppermute | solution.py:271
  90.1 1.8 copy-start.1
  98.1 7.4 %copy-start.5 = (s32[16,4,8]{0,2,1:T(8,128)S(1)}, s32[16,4,8]{0,2,1:T(8,128)}, u32[]{:S(2)}) copy-start(s32[16,4,8]{0,2,1:T(8,128)} %param.17) | copy-start | bytes 6148
  98.1 36.0 %all-to-all-start.1 = ((bf16[16,16,4096]{2,1,0:T(8,128)(2,1)}), bf16[16,16,4096]{2,1,0:T(8,128)(2,1)S(1)}, u32[]{:S(2)}, u32[]{:S(2)}) async-start(bf16[16,16,4096]{2,1,0:T(8,128)(2,1)} %bitcast.10), calls=%async_computation.1 | async-start | bytes 4194304 | tf_op jit(solution)/shard_map/all_to_all | solution.py:286
  106.2 28.2 %copy-start.3 = (bf16[16,4,4096]{2,1,0:T(4,128)(2,1)S(1)}, bf16[16,4,4096]{2,1,0:T(4,128)(2,1)}, u32[]{:S(2)}) copy-start(bf16[16,4,4096]{2,1,0:T(4,128)(2,1)} %param.14) | copy-start | bytes 1572868
  134.4 0.7 copy-start.4
  223.6 2.0 copy-start
  225.6 6.2 %copy-start.6 = (f32[16,4,8]{0,2,1:T(8,128)S(1)}, f32[16,4,8]{0,2,1:T(8,128)}, u32[]{:S(2)}) copy-start(f32[16,4,8]{0,2,1:T(8,128)} %param.18) | copy-start | bytes 6148
  225.6 58.4 %all-to-all-start.3 = ((bf16[128,8,2048]{2,1,0:T(8,128)(2,1)}), bf16[128,8,2048]{2,1,0:T(8,128)(2,1)}, u32[]{:S(2)}, u32[]{:S(2)}) async-start(bf16[128,8,2048]{2,1,0:T(8,128)(2,1)} %bitcast.62), calls=%async_computation.3 | async-start | bytes 8388608 | tf_op jit(solution)/shard_map/all_to_all | solution.py:313

commit v2 on v1

v2 whole, which is shorter than its diff:
```python
import jax
import jax.numpy as jnp
from jax import lax
from jax.experimental import pallas as pl
from jax.experimental.pallas import tpu as pltpu
from jax.sharding import Mesh
from jax.sharding import PartitionSpec as P

HEAD = 128
TOPK = 8
CTX = ("x", "zl")
EXP = ("zh", "yh", "yl", "core")
ALL = CTX + EXP
QUAD = ("yl", "core")
SHAPE = (4, 2, 2, 2, 2, 2)
LOG2E = 1.4426950408889634
F32 = jnp.float32
BF16 = jnp.bfloat16
NEG = -1e30
CHUNKS = 6
VMEM = 40 * 1024 * 1024
VMEM_SMALL = 24 * 1024 * 1024


def cost(microseconds):
    return pl.CostEstimate(
        flops=int(microseconds * 1.1e9), bytes_accessed=1 << 20, transcendentals=0
    )


def nt(a, b):
    return lax.dot_general(a, b, (((1,), (1,)), ((), ())), preferred_element_type=F32)


def tn(a, b):
    return lax.dot_general(a, b, (((0,), (0,)), ((), ())), preferred_element_type=F32)


def attention_kernel(ctx_ref, *refs):
    q_hbm, kv_ref, out_refs = refs[:CHUNKS], refs[CHUNKS], refs[CHUNKS + 1 : CHUNKS + 3]
    q_refs, top_ref, sum_ref, acc_ref, sem = refs[CHUNKS + 3 :]
    loads = [pltpu.make_async_copy(q_hbm[c], q_refs.at[c], sem.at[c]) for c in range(CHUNKS)]
    for load in loads:
        load.start()
    for load in loads:
        load.wait()
    ctx = ctx_ref[0]
    length = kv_ref.shape[1]
    rows = 2 * length
    factor = HEAD**-0.5 * LOG2E

    def block(index, count, first):
        kv = kv_ref[pl.ds(index, count)].reshape(count * length, 2 * HEAD)
        key, value = kv[:, :HEAD], kv[:, HEAD:]
        for c in range(CHUNKS):
            query = jnp.concatenate([q_refs[c, :, :HEAD], q_refs[c, :, HEAD:]], axis=0)
            scores = nt(key, query)
            if first:
                shape = (count * length, rows)
                key_pos = lax.broadcasted_iota(jnp.int32, shape, 0) - (count - 1) * length
                query_pos = lax.broadcasted_iota(jnp.int32, shape, 1) % length
                scores = jnp.where(key_pos <= query_pos, scores, NEG)
            new = jnp.max(scores, axis=0, keepdims=True)
            if not first:
                old = top_ref[c]
                new = jnp.maximum(old, new)
            weights = jnp.exp2((scores - new) * factor)
            total = jnp.sum(weights, axis=0, keepdims=True)
            part = tn(value, weights.astype(BF16))
            if not first:
                shrink = jnp.exp2((old - new) * factor)
                total = total + sum_ref[c] * shrink
                part = part + acc_ref[c] * shrink
            sum_ref[c] = total
            acc_ref[c] = part
            top_ref[c] = new

    @pl.when(ctx % 2 == 1)
    def _():
        block(ctx - 1, 2, True)

    @pl.when(ctx % 2 == 0)
    def _():
        block(ctx, 1, True)

    @pl.loop(0, ctx // 2)
    def _(index):
        block(index * 2, 2, False)

    for c in range(CHUNKS):
        done = (acc_ref[c] / sum_ref[c]).T.astype(BF16)
        out_ref, start = out_refs[c % 2], c // 2 * 256
        out_ref[:, start : start + HEAD] = done[:length]
        out_ref[:, start + HEAD : start + 256] = done[length:]


def attention(ctx, chunks, kv):
    length = kv.shape[1]
    vmem = pl.BlockSpec(memory_space=pltpu.VMEM)
    return pl.pallas_call(
        attention_kernel,
        out_shape=(jax.ShapeDtypeStruct((length, 128 * CHUNKS), BF16),) * 2,
        in_specs=[pl.BlockSpec(memory_space=pltpu.SMEM)]
        + [pl.BlockSpec(memory_space=pl.ANY)] * CHUNKS
        + [vmem],
        out_specs=(vmem, vmem),
        scratch_shapes=[
            pltpu.VMEM((CHUNKS, length, 2 * HEAD), BF16),
            pltpu.VMEM((CHUNKS, 1, 2 * length), F32),
            pltpu.VMEM((CHUNKS, 1, 2 * length), F32),
            pltpu.VMEM((CHUNKS, HEAD, 2 * length), F32),
            pltpu.SemaphoreType.DMA((CHUNKS,)),
        ],
        compiler_params=pltpu.CompilerParams(vmem_limit_bytes=VMEM_SMALL),
        cost_estimate=cost(0.1),
        name="attention",
    )(ctx, *(pltpu.with_memory_space_constraint(q, pltpu.HBM) for q in chunks), kv)


def project_kernel(core_ref, own0_ref, own1_ref, other0_ref, other1_ref, *refs):
    first, second, out_ref = refs[:4], refs[4:8], refs[8]
    core = core_ref[0]
    length = own0_ref.shape[0]
    own_refs, other_refs = (own0_ref, own1_ref), (other0_ref, other1_ref)
    tile = out_ref.shape[3]
    steps = pl.num_programs(0)

    def run(parts):
        total = None
        for c, w_ref in parts:
            rows = jnp.concatenate(
                [
                    own_refs[c % 2][:, 256 * (c // 2) : 256 * (c // 2 + 1)],
                    other_refs[1 - c % 2][:, 256 * (c // 2) : 256 * (c // 2 + 1)],
                ],
                axis=0,
            )
            part = jnp.dot(rows, w_ref[...], preferred_element_type=F32)
            total = part if total is None else total + part
        total = total.astype(BF16)
        out_ref[:, core] = total[:length].reshape(-1, 16, tile)
        out_ref[:, 1 - core] = total[length:].reshape(-1, 16, tile)

    @pl.when(pl.program_id(0) < steps // 2)
    def _():
        run(zip((0, 1, 2, 3), first))

    @pl.when(pl.program_id(0) >= steps // 2)
    def _():
        run(zip((0, 1, 4, 5), second))


def project(core, own, other, first, second):
    rows, width = own[0].shape[0], first[0].shape[1]
    tile = 512
    steps = 2 * width // tile
    att = pl.BlockSpec(own[0].shape, lambda i: (0, 0))
    in_first = pl.BlockSpec((256, tile), lambda i: (0, jnp.minimum(i, steps // 2 - 1)))
    in_second = pl.BlockSpec((256, tile), lambda i: (0, jnp.maximum(i - steps // 2, 0)))
    return pl.pallas_call(
        project_kernel,
        grid=(steps,),
        out_shape=pltpu.HBM((rows // 16, 2, 16, 2 * width), BF16),
        in_specs=[pl.BlockSpec(memory_space=pltpu.SMEM)]
        + [att] * 4
        + [in_first] * 4
        + [in_second] * 4,
        out_specs=pl.BlockSpec((rows // 16, 2, 16, tile), lambda i: (0, 0, 0, i)),
        compiler_params=pltpu.CompilerParams(vmem_limit_bytes=VMEM_SMALL),
        cost_estimate=cost(0.1),
        name="project",
    )(core, *own, *other, *first, *second)


def norm_kernel(parts_ref, res_ref, gain_ref, dispatch_ref, out_ref, stream_ref, x_ref):
    groups, _, _, _, positions, half = parts_ref.shape
    squares = {}
    for s in range(4):
        rows = slice(positions * s, positions * (s + 1))
        total = None
        for h in range(2):
            value = res_ref[h, rows].astype(F32)
            for g in range(groups):
                value = value + parts_ref[g, s // 2, h, s % 2].astype(F32)
            value = value.astype(BF16)
            stream_ref[h, rows] = value
            value = value.astype(F32)
            part = jnp.sum(value * value, axis=1, keepdims=True)
            total = part if total is None else total + part
        squares[s] = lax.rsqrt(total / (2 * half) + 1e-06)
    for s in range(4):
        rows = slice(positions * s, positions * (s + 1))
        for h in range(2):
            value = stream_ref[h, rows].astype(F32) * squares[s] * gain_ref[h]
            x_ref[64 * h + positions * s : 64 * h + positions * (s + 1)] = value.astype(BF16)

    @pl.loop(0, half // 512)
    def _(i):
        cols = pl.ds(pl.multiple_of(i * 512, 512), 512)
        out_ref[:, cols] = jnp.dot(
            dispatch_ref[...], x_ref[:, cols], preferred_element_type=F32
        ).astype(BF16)


def norm_dispatch(parts, held, gain, dispatch):
    half = held.shape[2]
    vmem = pl.BlockSpec(memory_space=pltpu.VMEM)
    return pl.pallas_call(
        norm_kernel,
        out_shape=(
            jax.ShapeDtypeStruct((dispatch.shape[0], half), BF16),
            jax.ShapeDtypeStruct(held.shape, BF16),
        ),
        in_specs=[vmem] * 4,
        out_specs=(vmem, vmem),
        scratch_shapes=[pltpu.VMEM((dispatch.shape[1], half), BF16)],
        compiler_params=pltpu.CompilerParams(vmem_limit_bytes=VMEM_SMALL),
        cost_estimate=cost(2.2),
        name="norm_dispatch",
    )(parts, held, gain, dispatch)


def combine_kernel(ret_ref, combine_ref, stream_ref, out_ref):
    tile = ret_ref.shape[1]
    half = out_ref.shape[1] // 2
    tokens = out_ref.shape[0]
    step = pl.program_id(0)
    mixture = jnp.dot(combine_ref[...], ret_ref[...], preferred_element_type=F32)
    mixture = mixture[: 2 * tokens] + mixture[2 * tokens :]
    to = lax.broadcasted_iota(jnp.int32, (tokens, tokens), 0)
    frm = lax.broadcasted_iota(jnp.int32, (tokens, tokens), 1)
    order = jnp.where(frm == (to % 4) * (tokens // 4) + to // 4, 1.0, 0.0).astype(BF16)
    for h in range(2):
        back = jnp.dot(order, stream_ref[h], preferred_element_type=F32)
        cols = pl.ds(pl.multiple_of(h * half + step * tile, tile), tile)
        out_ref[:, cols] = (back + mixture[tokens * h : tokens * (h + 1)]).astype(BF16)


def combine_rows(returned, combine, stream):
    rows, half = returned.shape
    tokens = stream.shape[1]
    tile = 512
    return pl.pallas_call(
        combine_kernel,
        grid=(half // tile,),
        out_shape=jax.ShapeDtypeStruct((tokens, 2 * half), BF16),
        in_specs=[
            pl.BlockSpec((rows, tile), lambda i: (0, i)),
            pl.BlockSpec(combine.shape, lambda i: (0, 0)),
            pl.BlockSpec((2, tokens, tile), lambda i: (0, 0, i)),
        ],
        out_specs=pl.BlockSpec((tokens, 2 * half), lambda i: (0, 0)),
        compiler_params=pltpu.CompilerParams(vmem_limit_bytes=VMEM_SMALL),
        cost_estimate=cost(4),
        name="combine",
    )(returned, combine, stream)


UP_TILE = 256
DOWN_TILE = 512
BLOCK = 256


def shuffle():
    r = lax.broadcasted_iota(jnp.int32, (BLOCK, BLOCK), 0)
    c = lax.broadcasted_iota(jnp.int32, (BLOCK, BLOCK), 1)
    half, r = r // 128, r % 128
    return jnp.where(c == (r // 4) * 8 + 4 * half + r % 4, 1.0, 0.0).astype(BF16)


def expert_kernel(
    r_ref, wg_hbm, wu_hbm, wd_hbm, out_hbm,
    x_ref, hid_ref, wg_ref, wu_ref, wd_ref, stage_ref, up_sem, down_sem, out_sem,
):
    rows, width = r_ref.shape
    ups = hid_ref.shape[1] // UP_TILE
    loads = []
    for i in range(ups):
        cols = slice(i * UP_TILE, (i + 1) * UP_TILE)
        loads.append(
            (
                pltpu.make_async_copy(wg_hbm.at[:, cols], wg_ref.at[i], up_sem.at[0, i]),
                pltpu.make_async_copy(wu_hbm.at[:, cols], wu_ref.at[i], up_sem.at[1, i]),
            )
        )
        for load in loads[-1]:
            load.start()
    load_down = pltpu.make_async_copy(wd_hbm, wd_ref, down_sem)
    load_down.start()
    matrix = shuffle()

    @pl.loop(0, rows // BLOCK)
    def _(b):
        block = r_ref[pl.ds(pl.multiple_of(b * BLOCK, BLOCK), BLOCK), :]
        moved = jnp.dot(matrix, block, preferred_element_type=F32).astype(BF16)
        to = pl.ds(pl.multiple_of(b * 128, 128), 128)
        x_ref[to, :width] = moved[:128]
        x_ref[to, width:] = moved[128:]

    for i in range(ups):
        for load in loads[i]:
            load.wait()
        x = x_ref[...]
        gate = jnp.dot(x, wg_ref[i], preferred_element_type=F32)
        up = jnp.dot(x, wu_ref[i], preferred_element_type=F32)
        hid_ref[:, i * UP_TILE : (i + 1) * UP_TILE] = (
            gate / (1.0 + jnp.exp(-gate)) * up
        ).astype(BF16)

    load_down.wait()
    stores = []
    for i in range(width // DOWN_TILE):
        cols = slice(i * DOWN_TILE, (i + 1) * DOWN_TILE)
        cols_high = slice(width + i * DOWN_TILE, width + (i + 1) * DOWN_TILE)
        hidden = hid_ref[...]
        low = jnp.dot(hidden, wd_ref[:, cols], preferred_element_type=F32).astype(BF16)
        high = jnp.dot(hidden, wd_ref[:, cols_high], preferred_element_type=F32).astype(BF16)
        for b in range(rows // BLOCK):
            part = slice(128 * b, 128 * (b + 1))
            both = jnp.concatenate([low[part], high[part]], axis=0)
            stage_ref[i, BLOCK * b : BLOCK * (b + 1), :] = tn(matrix, both).astype(BF16)
        store = pltpu.make_async_copy(stage_ref.at[i], out_hbm.at[:, cols], out_sem.at[i])
        store.start()
        stores.append(store)
    for store in stores:
        store.wait()


def experts(arrived, w_gate, w_up, w_down):
    rows, width = arrived.shape
    hidden = w_down.shape[0]
    ups, downs = hidden // UP_TILE, width // DOWN_TILE
    hbm = pl.BlockSpec(memory_space=pl.ANY)
    return pl.pallas_call(
        expert_kernel,
        out_shape=pltpu.HBM((rows, width), BF16),
        in_specs=[pl.BlockSpec(memory_space=pltpu.VMEM)] + [hbm] * 3,
        out_specs=hbm,
        scratch_shapes=[
            pltpu.VMEM((rows // 2, 2 * width), BF16),
            pltpu.VMEM((rows // 2, hidden), BF16),
            pltpu.VMEM((ups, 2 * width, UP_TILE), BF16),
            pltpu.VMEM((ups, 2 * width, UP_TILE), BF16),
            pltpu.VMEM(w_down.shape, BF16),
            pltpu.VMEM((downs, rows, DOWN_TILE), BF16),
            pltpu.SemaphoreType.DMA((2, ups)),
            pltpu.SemaphoreType.DMA,
            pltpu.SemaphoreType.DMA((downs,)),
        ],
        compiler_params=pltpu.CompilerParams(vmem_limit_bytes=VMEM),
        cost_estimate=cost(14),
        name="experts",
    )(
        pltpu.with_memory_space_constraint(arrived, pltpu.VMEM),
        *(pltpu.with_memory_space_constraint(w, pltpu.HBM) for w in (w_gate, w_up, w_down)),
    )


def routing(expert_ids, expert_gates, experts_all, capacity):
    positions, sequences, _ = expert_ids.shape
    tokens = positions * sequences
    flat_ids = expert_ids.reshape(-1)
    onehot = (flat_ids[:, None] == jnp.arange(experts_all, dtype=jnp.int32)[None, :]).astype(
        jnp.int32
    )
    before = jnp.cumsum(onehot, axis=0) - onehot
    slot = jnp.sum(before * onehot, axis=1)
    place = (flat_ids * 2 * capacity + slot).reshape(tokens, TOPK)
    rows = jnp.arange(2 * capacity * experts_all, dtype=jnp.int32)
    place_sp = place.reshape(positions, sequences, TOPK).transpose(1, 0, 2).reshape(tokens, TOPK)

    def dispatch_half(half):
        hit = rows[:, None, None] == place_sp[None] + half * capacity
        return jnp.any(hit, axis=2)

    dispatch = jnp.concatenate([dispatch_half(0), dispatch_half(1)], axis=1).astype(BF16)
    gates = expert_gates.reshape(tokens, TOPK)

    def combine_half(half):
        hit = rows[None, None, :] == (place + half * capacity)[:, :, None]
        return jnp.sum(jnp.where(hit, gates[:, :, None], 0.0), axis=1)

    combine = jnp.concatenate([combine_half(0), combine_half(1)], axis=0)
    high = combine.astype(BF16)
    low = (combine - high.astype(F32)).astype(BF16)
    return dispatch, jnp.concatenate([high, low], axis=0)


def local(
    queries,
    keys,
    values,
    residual,
    out_weight,
    norm_gain,
    expert_ids,
    expert_gates,
    w_gate,
    w_up,
    w_down,
):
    ctx_index = lax.axis_index(CTX)
    zh = lax.axis_index("zh")
    core = lax.axis_index("core")
    quad = lax.axis_index(QUAD)
    quad_count = lax.axis_size(QUAD)
    ctx_count = lax.axis_size(CTX)
    exp_count = lax.axis_size(EXP)
    sequences, length, _ = queries.shape
    width = residual.shape[2]

    def mine(a):
        a = lax.dynamic_index_in_dim(a, quad, 0, False)
        return lax.dynamic_slice_in_dim(a, zh * HEAD, HEAD, 1)

    kv_mine = jnp.concatenate([mine(keys), mine(values)], axis=1)
    kv_send = jnp.broadcast_to(kv_mine[None], (ctx_count,) + kv_mine.shape)

    half = width // 2
    part = half // 2
    ring = ("yh", "yl", "core")
    pairs = {m: [(i, i ^ m) for i in range(8)] for m in range(8)}
    chunks = [lax.dynamic_index_in_dim(queries, quad, 0, False)]
    for m in (1, 2, 3, 6, 7):
        chunk = lax.dynamic_index_in_dim(queries, quad ^ (m & 3), 0, False)
        chunks.append(lax.ppermute(chunk, ring, pairs[m]))

    def columns(of_core, second):
        start = of_core * half + (part if second else 0)
        return lax.dynamic_slice_in_dim(out_weight, start, part, 1)

    mine_a, mine_b, swap_a, swap_b, _ = lax.optimization_barrier(
        (
            columns(core, False),
            columns(core, True),
            columns(1 - core, False),
            columns(1 - core, True),
            chunks[1:],
        )
    )
    first = [mine_a] + [
        lax.ppermute(w, ring, pairs[m]) for w, m in ((swap_a, 1), (mine_a, 2), (swap_a, 3))
    ]
    second = [mine_b] + [
        lax.ppermute(w, ring, pairs[m]) for w, m in ((swap_b, 1), (mine_b, 6), (swap_b, 7))
    ]

    kv = lax.all_to_all(kv_send, CTX, 0, 0, tiled=True)
    attended = attention(ctx_index[None].astype(jnp.int32), chunks, kv)
    attended_other = [lax.ppermute(a, "core", [(0, 1), (1, 0)]) for a in attended]
    partial_sums = project(core[None].astype(jnp.int32), attended, attended_other, first, second)
    parts = lax.all_to_all(partial_sums, EXP, 0, 0, tiled=True)
    positions = length // exp_count
    tokens = sequences * positions
    parts = parts.reshape(exp_count // quad_count, 2, 2, 2, positions, half)
    held = residual.reshape(positions, sequences, 2, half).transpose(2, 1, 0, 3)
    held = held.reshape(2, tokens, half)

    experts_all = w_gate.shape[0] * ctx_count * exp_count
    capacity = tokens * TOPK // experts_all
    dispatch, combine = routing(expert_ids, expert_gates, experts_all, capacity)
    outgoing, stream = norm_dispatch(parts, held, norm_gain.reshape(2, 1, half), dispatch)
    arrived = lax.all_to_all(
        outgoing.reshape(experts_all, 2 * capacity, half), ALL, 0, 0, tiled=True
    )
    produced = experts(
        arrived.reshape(experts_all * 2 * capacity, half), w_gate[0], w_up[0], w_down[0]
    )
    returned = lax.all_to_all(
        produced.reshape(experts_all, 2 * capacity, half), ALL, 0, 0, tiled=True
    )
    out = combine_rows(
        returned.reshape(experts_all * 2 * capacity, half), combine, stream
    )
    return out.reshape(residual.shape)


def solution(mesh):
    fine = Mesh(mesh.devices.reshape(SHAPE), ALL)
    rows = P(ALL, None, None)
    in_specs = (
        P(None, CTX, EXP),
        P(None, CTX, None),
        P(None, CTX, None),
        rows,
        P(EXP, None),
        P(),
        rows,
        rows,
        rows,
        rows,
        rows,
    )
    return jax.shard_map(local, mesh=fine, in_specs=in_specs, out_specs=rows, check_vma=False)
```

time: 290 us -> 232 us (0.80)
  waiting for transfers between devices: 149 us -> 92.1 us
  blocking collectives: 68.3 us -> 60.9 us
  matrix products: 4.74 us -> 0 us
  Pallas kernels: 26.6 us -> 30.2 us
  starting transfers between devices: 28.2 us -> 31.5 us
  local copies, waits for them, and re-layouts: 7.69 us -> 10.6 us
    ppermute x6 -> x13, waiting for transfers between devices: 72.3 us -> 19.8 us  [the longest x6 17 us: local(): lax.ppermute(w, ring, pairs[m])]
    all_to_all x1, blocking collectives: 68.3 us -> 60.9 us  [local(): lax.all_to_all(outgoing.reshape(experts_all, 2 * capacity, half), ALL, 0,...]
    dot_general x2 -> x0, matrix products: 4.74 us -> none  [the longest x1 3.43 us: local(): jnp.dot(combine, returned.reshape(experts_all * 2 * capacity, half), pref...]
    dynamic_slice x1 -> x2, local copies, waits for them, and re-layouts: 0.04 us -> 3.89 us  [the longest x1 2.76 us: columns(): return lax.dynamic_slice_in_dim(out_weight, start, part, 1)]
    all_to_all x1, waiting for transfers between devices: 25.8 us -> 22 us  [local(): parts = lax.all_to_all(partial_sums, EXP, 0, 0, tiled=True)]
    pallas_call x3 -> x5, Pallas kernels: 26.6 us -> 30.2 us  [the longest x1 15 us: experts(): pl.pallas_call(expert_kernel, out_shape=pltpu.HBM((rows, width), BF16), i...]
    ppermute x6 -> x13, starting transfers between devices: 10.9 us -> 13.5 us  [the longest x5 5.72 us: local(): chunks.append(lax.ppermute(chunk, ring, pairs[m]))]
  transfers between devices with their start and end apart: 9 -> 16, of which waited for: 5 -> 7; matrix products, arithmetic and copies ran while one was open for 3% -> 5% of each run, Pallas kernels for 1% -> 2%
where the time goes in v2:
time: 232 us; the launch traced here: 231 us
  waiting for transfers between devices  92.1 us (40%)
  blocking collectives  60.9 us (26%)
  starting transfers between devices  31.5 us (14%)
  Pallas kernels  30.2 us (13%)
  local copies, waits for them, and re-layouts  10.6 us (5%)
  other arithmetic  5.36 us (2%)
    all_to_all x1, blocking collectives, local(): lax.all_to_all(outgoing.reshape(experts_all, 2 * capacity, half), ALL, 0,...  60.9 us
    all_to_all x1, waiting for transfers between devices, local(): lax.all_to_all(produced.reshape(experts_all, 2 * capacity, half), ALL, 0,...  50.3 us
    all_to_all x1, waiting for transfers between devices, local(): parts = lax.all_to_all(partial_sums, EXP, 0, 0, tiled=True)  22 us
    ppermute x6, waiting for transfers between devices, local(): lax.ppermute(w, ring, pairs[m])  17 us
    pallas_call x1, Pallas kernels, experts(): pl.pallas_call(expert_kernel, out_shape=pltpu.HBM((rows, width), BF16), i...  15 us
    all_to_all x1, starting transfers between devices, local(): kv = lax.all_to_all(kv_send, CTX, 0, 0, tiled=True)  6.2 us
    all_to_all x1, starting transfers between devices, local(): parts = lax.all_to_all(partial_sums, EXP, 0, 0, tiled=True)  6.14 us
    ppermute x5, starting transfers between devices, local(): chunks.append(lax.ppermute(chunk, ring, pairs[m]))  5.72 us
  transfers between devices with their start and end apart: 16, of which 7 were waited for; matrix products, arithmetic and copies ran while one was open for 5% of the time, Pallas kernels for 2%

profile of v2, /device:TPU:1, one launch (start us, length us, event | category | flops | bytes accessed | tf_op | source)
XLA Modules:
  0.0 231.0 jit_solution(11188557483076301307)
XLA Ops:
  0.0 1.1 dynamic-slice_bitcast_fusion.4
  1.2 1.0 broadcast_in_dim.38
  2.2 6.2 %all-to-all-start = ((bf16[8,256,256]{2,1,0:T(8,128)(2,1)}), bf16[8,256,256]{2,1,0:T(8,128)(2,1)S(1)}, u32[]{:S(2)}, u32[]{:S(2)}) async-start(bf16[8,256,256]{2,1,0:T(8,128)(2,1)} %broadcast_in_dim.38), calls=%async_computation | async-start | bytes 2097152 | tf_op jit(solution)/shard_map/all_to_all | solution.py:448
  8.4 0.7 dynamic-slice_bitcast_fusion
  9.1 1.3 collective-permute-start.1
  10.4 1.9 collective-permute-start.3
  12.3 1.8 collective-permute-start.2
  14.1 0.4 collective-permute-start.4
  14.5 0.3 collective-permute-start
  14.8 2.8 %constant_dynamic-slice_fusion = (bf16[256,1024]{1,0:T(8,128)(2,1)}, bf16[256,1024]{1,0:T(8,128)(2,1)S(1)}, bf16[256,1024]{1,0:T(8,128)(2,1)S(1)}, bf16[256,1024]{1,0:T(8,128)(2,1)}) fusion(bf16[256,4096]{1,0:T(8,128)(2,1)} %param.15, s32[]{:T(128)S(6)} %select_n.54, s32[]{:T(128)S(6)} %select_n.52, s32[]{:T(128)S(6)} %select_n.51, s32[]{:T(128)S(6)} %select_n.53), kind=kLoop, calls=%fused_computation.31 | loop fusion | bytes 4194320 | tf_op jit(solution)/shard_map/dynamic_slice | solution.py:430
  17.6 0.1 collective-permute-done.2.refs_3_
  17.7 2.7 %collective-permute-done.4.refs_5_ = bf16[256,256]{1,0:T(8,128)(2,1)S(1)} collective-permute-done((bf16[256,256]{1,0:T(8,128)(2,1)S(1)}, bf16[256,256]{1,0:T(8,128)(2,1)S(1)}, u32[]{:S(2)}, u32[]{:S(2)}) %collective-permute-start.4) | collective-permute-done | bytes 131104 | tf_op jit(solution)/shard_map/ppermute | solution.py:426
  20.4 0.6 copy-done.7
  21.1 1.4 collective-permute-start.11
  22.5 1.9 collective-permute-start.12
  24.5 2.1 collective-permute-start.9
  26.6 3.5 %attention.1 = (bf16[256,768]{1,0:T(8,128)(2,1)S(1)}, bf16[256,768]{1,0:T(8,128)(2,1)S(1)}) custom-call(s32[1]{0:T(128)} %bitcast.1.ctx_ref, bf16[256,256]{1,0:T(8,128)(2,1)} %get-tuple-element.31.refs_0_, bf16[256,256]{1,0:T(8,128)(2,1)} %copy-done.8, bf16[256,256]{1,0:T(8,128)(2,1)} %copy-done.4, bf16[256,256]{1,0:T(8,128)(2,1)} %copy-done.6, ...), custom_call_target="tpu_custom_call" | custom-call | flops 110000000 | bytes 1048576 | tf_op jit(solution)/shard_map/attention/pallas_call | solution.py:100
  30.2 5.1 %collective-permute-done.11.refs_6_ = bf16[256,1024]{1,0:T(8,128)(2,1)S(1)} collective-permute-done((bf16[256,1024]{1,0:T(8,128)(2,1)S(1)}, bf16[256,1024]{1,0:T(8,128)(2,1)S(1)}, u32[]{:S(2)}, u32[]{:S(2)}) %collective-permute-start.11) | collective-permute-done | bytes 524320 | tf_op jit(solution)/shard_map/ppermute | solution.py:445
  35.3 2.3 %collective-permute-start.5 = (bf16[256,768]{1,0:T(8,128)(2,1)S(1)}, bf16[256,768]{1,0:T(8,128)(2,1)S(1)}, u32[]{:S(2)}, u32[]{:S(2)}) collective-permute-start(bf16[256,768]{1,0:T(8,128)(2,1)S(1)} %get-tuple-element.13.own0_ref), channel_id=1, source_target_pairs={{0,1},{1,0},{2,3},{3,2},{4,5},{5,4},{6,7},{7,6},{8,9},{9,8},{10,11... | collective-permute-start | bytes 1179656 | tf_op jit(solution)/shard_map/ppermute | solution.py:450
  37.6 9.7 %collective-permute-done.12.refs_7_ = bf16[256,1024]{1,0:T(8,128)(2,1)} collective-permute-done((bf16[256,1024]{1,0:T(8,128)(2,1)}, bf16[256,1024]{1,0:T(8,128)(2,1)}, u32[]{:S(2)}, u32[]{:S(2)}) %collective-permute-start.12) | collective-permute-done | bytes 524320 | tf_op jit(solution)/shard_map/ppermute | solution.py:445
  47.3 2.1 collective-permute-done.9.refs_3_
  49.4 5.5 %project.1 = bf16[16,2,16,2048]{3,2,1,0:T(8,128)(2,1)} custom-call(s32[1]{0:T(128)} %bitcast.core_ref, bf16[256,768]{1,0:T(8,128)(2,1)S(1)} %get-tuple-element.13.own0_ref, bf16[256,768]{1,0:T(8,128)(2,1)S(1)} %get-tuple-element.14.own1_ref, bf16[256,768]{1,0:T(8,128)(2,1)S(1)} %collective-permute-done.5.other0_ref, ...), custom_call_target="tpu_custom_call" | custom-call | flops 110000000 | bytes 1048576 | tf_op jit(solution)/shard_map/project/pallas_call | solution.py:160
  54.9 6.1 %all-to-all-start.1 = ((bf16[16,2,16,2048]{3,2,1,0:T(8,128)(2,1)}), bf16[16,2,16,2048]{3,2,1,0:T(8,128)(2,1)S(1)}, u32[]{:S(2)}, u32[]{:S(2)}) async-start(bf16[16,2,16,2048]{3,2,1,0:T(8,128)(2,1)} %project.1), calls=%async_computation.1 | async-start | bytes 4194304 | tf_op jit(solution)/shard_map/all_to_all | solution.py:452
  61.1 0.1 eq.84
  61.3 0.1 eq.80
  61.4 0.1 copy.31
  61.5 0.2 fusion.5
  61.8 0.2 fusion.4
  62.0 0.1 reduce_sum.32
  62.1 0.6 broadcast_multiply_fusion
  62.9 0.1 copy.34
  63.1 0.7 fusion.1
  63.8 0.3 copy.37
  64.1 0.7 fusion
  64.8 0.9 copy.36
  65.7 0.5 reshape.81
  66.2 0.3 copy.27
  66.5 1.1 add_convert_fusion.dispatch_ref
  67.6 22.0 %all-to-all-done.1 = bf16[16,2,16,2048]{3,2,1,0:T(8,128)(2,1)S(1)} async-done(((bf16[16,2,16,2048]{3,2,1,0:T(8,128)(2,1)}), bf16[16,2,16,2048]{3,2,1,0:T(8,128)(2,1)S(1)}, u32[]{:S(2)}, u32[]{:S(2)}) %all-to-all-start.1) | async-done | bytes 2097184 | tf_op jit(solution)/shard_map/all_to_all | solution.py:452
  89.6 2.2 norm_dispatch.1
  91.8 60.9 %all_to_all.20 = bf16[128,8,2048]{2,1,0:T(8,128)(2,1)S(1)} all-to-all(bf16[128,8,2048]{2,1,0:T(8,128)(2,1)S(1)} %bitcast.45), channel_id=1, replica_groups=mesh['x'=4,'zl'=2,'zh'=2,'yh'=2,'yl'=2,'core'=2] {'x','zl','zh','yh','yl..., dimensions={0} | all-to-all | bytes 8388608 | tf_op jit(solution)/shard_map/all_to_all | solution.py:463
  152.8 15.0 %experts.1 = bf16[1024,2048]{1,0:T(8,128)(2,1)} custom-call(bf16[1024,2048]{1,0:T(8,128)(2,1)S(1)} %bitcast.46, bf16[4096,768]{1,0:T(8,128)(2,1)} %bitcast.56, bf16[4096,768]{1,0:T(8,128)(2,1)} %bitcast.57, bf16[768,4096]{1,0:T(8,128)(2,1)} %bitcast.58), custom_call_target="tpu_custom_call" | custom-call | flops 15399999488 | bytes 1048576 | tf_op jit(solution)/shard_map/experts/pallas_call | solution.py:334
  167.8 5.6 %all-to-all-start.3 = ((bf16[128,8,2048]{2,1,0:T(8,128)(2,1)}), bf16[128,8,2048]{2,1,0:T(8,128)(2,1)}, u32[]{:S(2)}, u32[]{:S(2)}) async-start(bf16[128,8,2048]{2,1,0:T(8,128)(2,1)} %bitcast.50), calls=%async_computation.3 | async-start | bytes 8388608 | tf_op jit(solution)/shard_map/all_to_all | solution.py:469
  173.8 0.1 copy.42
  174.0 1.6 select_reduce_fusion.1
  175.7 50.3 %all-to-all-done.3 = bf16[128,8,2048]{2,1,0:T(8,128)(2,1)} async-done(((bf16[128,8,2048]{2,1,0:T(8,128)(2,1)}), bf16[128,8,2048]{2,1,0:T(8,128)(2,1)}, u32[]{:S(2)}, u32[]{:S(2)}) %all-to-all-start.3) | async-done | bytes 4194336 | tf_op jit(solution)/shard_map/all_to_all | solution.py:469
  226.1 4.0 %combine.1 = bf16[64,4096]{1,0:T(8,128)(2,1)S(1)} custom-call(bf16[1024,2048]{1,0:T(8,128)(2,1)} %bitcast.22.ret_ref, bf16[256,1024]{1,0:T(8,128)(2,1)S(1)} %pad_maximum_fusion.1.combine_ref, bf16[2,64,2048]{2,1,0:T(8,128)(2,1)S(1)} %get-tuple-element.20.stream_ref), custom_call_target="tpu_custom_call" | custom-call | flops 4400000000 | bytes 1048576 | tf_op jit(solution)/shard_map/combine/pallas_call | solution.py:243
  230.0 1.0 reshape.89
  (59 shorter events, 1.0 us)
Async XLA Ops:
  0.0 8.4 %copy-start.1 = (bf16[4,256,256]{2,1,0:T(8,128)(2,1)S(1)}, bf16[4,256,256]{2,1,0:T(8,128)(2,1)}, u32[]{:S(2)}) copy-start(bf16[4,256,256]{2,1,0:T(8,128)(2,1)} %param.11) | copy-start | bytes 1572868
  2.2 24.4 %all-to-all-start = ((bf16[8,256,256]{2,1,0:T(8,128)(2,1)}), bf16[8,256,256]{2,1,0:T(8,128)(2,1)S(1)}, u32[]{:S(2)}, u32[]{:S(2)}) async-start(bf16[8,256,256]{2,1,0:T(8,128)(2,1)} %broadcast_in_dim.38), calls=%async_computation | async-start | bytes 2097152 | tf_op jit(solution)/shard_map/all_to_all | solution.py:448
  9.1 8.5 %collective-permute-start.1 = (bf16[256,256]{1,0:T(8,128)(2,1)S(1)}, bf16[256,256]{1,0:T(8,128)(2,1)S(1)}, u32[]{:S(2)}, u32[]{:S(2)}) collective-permute-start(bf16[256,256]{1,0:T(8,128)(2,1)S(1)} %get-tuple-element.32), channel_id=1, source_target_pairs={{0,2},{1,3},{2,0},{3,1},{4,6},{5,7},{6,4},{7,5},{8,10},{9,11},{10,... | collective-permute-start | bytes 393224 | tf_op jit(solution)/shard_map/ppermute | solution.py:426
  10.4 7.3 %collective-permute-start.3 = (bf16[256,256]{1,0:T(8,128)(2,1)S(1)}, bf16[256,256]{1,0:T(8,128)(2,1)S(1)}, u32[]{:S(2)}, u32[]{:S(2)}) collective-permute-start(bf16[256,256]{1,0:T(8,128)(2,1)S(1)} %get-tuple-element.32), channel_id=1, source_target_pairs={{0,6},{1,7},{2,4},{3,5},{4,2},{5,3},{6,0},{7,1},{8,14},{9,15},{10,... | collective-permute-start | bytes 393224 | tf_op jit(solution)/shard_map/ppermute | solution.py:426
  12.3 5.4 %collective-permute-start.2 = (bf16[256,256]{1,0:T(8,128)(2,1)S(1)}, bf16[256,256]{1,0:T(8,128)(2,1)S(1)}, u32[]{:S(2)}, u32[]{:S(2)}) collective-permute-start(bf16[256,256]{1,0:T(8,128)(2,1)S(1)} %get-tuple-element.29), channel_id=1, source_target_pairs={{0,3},{1,2},{2,1},{3,0},{4,7},{5,6},{6,5},{7,4},{8,11},{9,10},{10,... | collective-permute-start | bytes 393224 | tf_op jit(solution)/shard_map/ppermute | solution.py:426
  14.1 6.3 %collective-permute-start.4 = (bf16[256,256]{1,0:T(8,128)(2,1)S(1)}, bf16[256,256]{1,0:T(8,128)(2,1)S(1)}, u32[]{:S(2)}, u32[]{:S(2)}) collective-permute-start(bf16[256,256]{1,0:T(8,128)(2,1)S(1)} %get-tuple-element.29), channel_id=1, source_target_pairs={{0,7},{1,6},{2,5},{3,4},{4,3},{5,2},{6,1},{7,0},{8,15},{9,14},{10,... | collective-permute-start | bytes 393224 | tf_op jit(solution)/shard_map/ppermute | solution.py:426
  14.5 3.1 %collective-permute-start = (bf16[256,256]{1,0:T(8,128)(2,1)S(1)}, bf16[256,256]{1,0:T(8,128)(2,1)S(1)}, u32[]{:S(2)}, u32[]{:S(2)}) collective-permute-start(bf16[256,256]{1,0:T(8,128)(2,1)S(1)} %get-tuple-element.30), channel_id=1, source_target_pairs={{0,1},{1,0},{2,3},{3,2},{4,5},{5,4},{6,7},{7,6},{8,9},{9,8},{10,11... | collective-permute-start | bytes 393224 | tf_op jit(solution)/shard_map/ppermute | solution.py:426
  17.6 2.9 %copy-start.8 = (bf16[256,256]{1,0:T(8,128)(2,1)}, bf16[256,256]{1,0:T(8,128)(2,1)S(1)}, u32[]{:S(2)}) copy-start(bf16[256,256]{1,0:T(8,128)(2,1)S(1)} %collective-permute-done.refs_1_) | copy-start | bytes 393220
  17.6 9.0 %copy-start.4 = (bf16[256,256]{1,0:T(8,128)(2,1)}, bf16[256,256]{1,0:T(8,128)(2,1)S(1)}, u32[]{:S(2)}) copy-start(bf16[256,256]{1,0:T(8,128)(2,1)S(1)} %collective-permute-done.1.refs_2_) | copy-start | bytes 393220
  17.7 8.9 %copy-start.6 = (bf16[256,256]{1,0:T(8,128)(2,1)}, bf16[256,256]{1,0:T(8,128)(2,1)S(1)}, u32[]{:S(2)}) copy-start(bf16[256,256]{1,0:T(8,128)(2,1)S(1)} %collective-permute-done.2.refs_3_) | copy-start | bytes 393220
  17.7 8.9 %copy-start.5 = (bf16[256,256]{1,0:T(8,128)(2,1)}, bf16[256,256]{1,0:T(8,128)(2,1)S(1)}, u32[]{:S(2)}) copy-start(bf16[256,256]{1,0:T(8,128)(2,1)S(1)} %collective-permute-done.3.refs_4_) | copy-start | bytes 393220
  20.4 0.7 copy-start.7
  21.1 3.4 %collective-permute-start.10 = (bf16[256,1024]{1,0:T(8,128)(2,1)}, bf16[256,1024]{1,0:T(8,128)(2,1)S(1)}, u32[]{:S(2)}, u32[]{:S(2)}) collective-permute-start(bf16[256,1024]{1,0:T(8,128)(2,1)} %get-tuple-element.18), channel_id=1, source_target_pairs={{0,1},{1,0},{2,3},{3,2},{4,5},{5,4},{6,7},{7,6},{8,9},{9,8},{10,11... | collective-permute-start | bytes 1572872 | tf_op jit(solution)/shard_map/ppermute | solution.py:445
  21.1 14.2 %collective-permute-start.11 = (bf16[256,1024]{1,0:T(8,128)(2,1)S(1)}, bf16[256,1024]{1,0:T(8,128)(2,1)S(1)}, u32[]{:S(2)}, u32[]{:S(2)}) collective-permute-start(bf16[256,1024]{1,0:T(8,128)(2,1)S(1)} %get-tuple-element.17.refs_4_), channel_id=1, source_target_pairs={{0,6},{1,7},{2,4},{3,5},{4,2},{5,3},{6,0},{7,1},{8,14},{9,15},{10,... | collective-permute-start | bytes 1572872 | tf_op jit(solution)/shard_map/ppermute | solution.py:445
  22.5 24.8 %collective-permute-start.12 = (bf16[256,1024]{1,0:T(8,128)(2,1)}, bf16[256,1024]{1,0:T(8,128)(2,1)}, u32[]{:S(2)}, u32[]{:S(2)}) collective-permute-start(bf16[256,1024]{1,0:T(8,128)(2,1)} %get-tuple-element.18), channel_id=1, source_target_pairs={{0,7},{1,6},{2,5},{3,4},{4,3},{5,2},{6,1},{7,0},{8,15},{9,14},{10,... | collective-permute-start | bytes 1572872 | tf_op jit(solution)/shard_map/ppermute | solution.py:445
  24.4 22.9 %collective-permute-start.7 = (bf16[256,1024]{1,0:T(8,128)(2,1)}, bf16[256,1024]{1,0:T(8,128)(2,1)}, u32[]{:S(2)}, u32[]{:S(2)}) collective-permute-start(bf16[256,1024]{1,0:T(8,128)(2,1)} %get-tuple-element.16), channel_id=1, source_target_pairs={{0,1},{1,0},{2,3},{3,2},{4,5},{5,4},{6,7},{7,6},{8,9},{9,8},{10,11... | collective-permute-start | bytes 1572872 | tf_op jit(solution)/shard_map/ppermute | solution.py:442
  24.5 22.9 %collective-permute-start.8 = (bf16[256,1024]{1,0:T(8,128)(2,1)S(1)}, bf16[256,1024]{1,0:T(8,128)(2,1)}, u32[]{:S(2)}, u32[]{:S(2)}) collective-permute-start(bf16[256,1024]{1,0:T(8,128)(2,1)S(1)} %get-tuple-element.15.refs_0_), channel_id=1, source_target_pairs={{0,2},{1,3},{2,0},{3,1},{4,6},{5,7},{6,4},{7,5},{8,10},{9,11},{10,... | collective-permute-start | bytes 1572872 | tf_op jit(solution)/shard_map/ppermute | solution.py:442
  24.5 25.0 %collective-permute-start.9 = (bf16[256,1024]{1,0:T(8,128)(2,1)}, bf16[256,1024]{1,0:T(8,128)(2,1)}, u32[]{:S(2)}, u32[]{:S(2)}) collective-permute-start(bf16[256,1024]{1,0:T(8,128)(2,1)} %get-tuple-element.16), channel_id=1, source_target_pairs={{0,3},{1,2},{2,1},{3,0},{4,7},{5,6},{6,5},{7,4},{8,11},{9,10},{10,... | collective-permute-start | bytes 1572872 | tf_op jit(solution)/shard_map/ppermute | solution.py:442
  35.3 14.2 %collective-permute-start.5 = (bf16[256,768]{1,0:T(8,128)(2,1)S(1)}, bf16[256,768]{1,0:T(8,128)(2,1)S(1)}, u32[]{:S(2)}, u32[]{:S(2)}) collective-permute-start(bf16[256,768]{1,0:T(8,128)(2,1)S(1)} %get-tuple-element.13.own0_ref), channel_id=1, source_target_pairs={{0,1},{1,0},{2,3},{3,2},{4,5},{5,4},{6,7},{7,6},{8,9},{9,8},{10,11... | collective-permute-start | bytes 1179656 | tf_op jit(solution)/shard_map/ppermute | solution.py:450
  47.3 2.1 collective-permute-start.6
  54.9 6.1 %copy-start.11 = (s32[16,4,8]{0,2,1:T(8,128)S(1)}, s32[16,4,8]{0,2,1:T(8,128)}, u32[]{:S(2)}) copy-start(s32[16,4,8]{0,2,1:T(8,128)} %param.17) | copy-start | bytes 6148
  54.9 34.7 %all-to-all-start.1 = ((bf16[16,2,16,2048]{3,2,1,0:T(8,128)(2,1)}), bf16[16,2,16,2048]{3,2,1,0:T(8,128)(2,1)S(1)}, u32[]{:S(2)}, u32[]{:S(2)}) async-start(bf16[16,2,16,2048]{3,2,1,0:T(8,128)(2,1)} %project.1), calls=%async_computation.1 | async-start | bytes 4194304 | tf_op jit(solution)/shard_map/all_to_all | solution.py:452
  61.1 4.6 %copy-start.2 = (bf16[16,4,4096]{2,1,0:T(4,128)(2,1)S(1)}, bf16[16,4,4096]{2,1,0:T(4,128)(2,1)}, u32[]{:S(2)}) copy-start(bf16[16,4,4096]{2,1,0:T(4,128)(2,1)} %param.14) | copy-start | bytes 1572868
  61.8 27.9 %copy-start = (f32[4096]{0:T(1024)S(1)}, f32[4096]{0:T(1024)}, u32[]{:S(2)}) copy-start(f32[4096]{0:T(1024)} %param.16) | copy-start | bytes 49156
  62.0 2.8 %copy-start.9 = (s32[512]{0:T(512)}, s32[512]{0:T(512)S(1)}, u32[]{:S(2)}) copy-start(s32[512]{0:T(512)S(1)} %fusion.4) | copy-start | bytes 6148
  167.8 5.7 %copy-start.10 = (s32[512]{0:T(512)S(1)}, s32[512]{0:T(512)}, u32[]{:S(2)}) copy-start(s32[512]{0:T(512)} %copy-done.9) | copy-start | bytes 6148
  167.8 5.8 %copy-start.3 = (s32[16,4,8]{2,1,0:T(4,128)S(1)}, s32[16,4,8]{2,1,0:T(4,128)}, u32[]{:S(2)}) copy-start(s32[16,4,8]{2,1,0:T(4,128)} %get-tuple-element.33) | copy-start | bytes 6148
  167.8 6.1 %copy-start.12 = (f32[16,4,8]{0,2,1:T(8,128)S(1)}, f32[16,4,8]{0,2,1:T(8,128)}, u32[]{:S(2)}) copy-start(f32[16,4,8]{0,2,1:T(8,128)} %param.18) | copy-start | bytes 6148
  167.8 58.2 %all-to-all-start.3 = ((bf16[128,8,2048]{2,1,0:T(8,128)(2,1)}), bf16[128,8,2048]{2,1,0:T(8,128)(2,1)}, u32[]{:S(2)}, u32[]{:S(2)}) async-start(bf16[128,8,2048]{2,1,0:T(8,128)(2,1)} %bitcast.50), calls=%async_computation.3 | async-start | bytes 8388608 | tf_op jit(solution)/shard_map/all_to_all | solution.py:469

commit v3 on v2

--- a/solution.py
+++ b/solution.py
@@ -239,7 +239,7 @@
 def combine_rows(returned, combine, stream):
     rows, half = returned.shape
     tokens = stream.shape[1]
-    tile = 512
+    tile = 1024
     return pl.pallas_call(
         combine_kernel,
         grid=(half // tile,),

time: 232 us -> 231 us (level)
  no operation moved by 1% of the time
where the time goes in v3:
time: 231 us; the launch traced here: 230 us
  waiting for transfers between devices  92.1 us (40%)
  blocking collectives  60.9 us (26%)
  starting transfers between devices  31.5 us (14%)
  Pallas kernels  29.4 us (13%)
  local copies, waits for them, and re-layouts  10.6 us (5%)
  other arithmetic  5.36 us (2%)
    all_to_all x1, blocking collectives, local(): lax.all_to_all(outgoing.reshape(experts_all, 2 * capacity, half), ALL, 0,...  60.9 us
    all_to_all x1, waiting for transfers between devices, local(): lax.all_to_all(produced.reshape(experts_all, 2 * capacity, half), ALL, 0,...  50.3 us
    all_to_all x1, waiting for transfers between devices, local(): parts = lax.all_to_all(partial_sums, EXP, 0, 0, tiled=True)  22 us
    ppermute x6, waiting for transfers between devices, local(): lax.ppermute(w, ring, pairs[m])  17 us
    pallas_call x1, Pallas kernels, experts(): pl.pallas_call(expert_kernel, out_shape=pltpu.HBM((rows, width), BF16), i...  15 us
    all_to_all x1, starting transfers between devices, local(): kv = lax.all_to_all(kv_send, CTX, 0, 0, tiled=True)  6.2 us
    all_to_all x1, starting transfers between devices, local(): parts = lax.all_to_all(partial_sums, EXP, 0, 0, tiled=True)  6.14 us
    ppermute x5, starting transfers between devices, local(): chunks.append(lax.ppermute(chunk, ring, pairs[m]))  5.72 us
  transfers between devices with their start and end apart: 16, of which 7 were waited for; matrix products, arithmetic and copies ran while one was open for 5% of the time, Pallas kernels for 2%

profile of v3, /device:TPU:1, one launch (start us, length us, event | category | flops | bytes accessed | tf_op | source)
XLA Modules:
  0.0 230.2 jit_solution(12019310739947273770)
XLA Ops:
  0.0 1.1 dynamic-slice_bitcast_fusion.4
  1.2 1.0 broadcast_in_dim.38
  2.2 6.2 %all-to-all-start = ((bf16[8,256,256]{2,1,0:T(8,128)(2,1)}), bf16[8,256,256]{2,1,0:T(8,128)(2,1)S(1)}, u32[]{:S(2)}, u32[]{:S(2)}) async-start(bf16[8,256,256]{2,1,0:T(8,128)(2,1)} %broadcast_in_dim.38), calls=%async_computation | async-start | bytes 2097152 | tf_op jit(solution)/shard_map/all_to_all | solution.py:448
  8.4 0.7 dynamic-slice_bitcast_fusion
  9.1 1.3 collective-permute-start.1
  10.4 1.9 collective-permute-start.3
  12.3 1.8 collective-permute-start.2
  14.1 0.4 collective-permute-start.4
  14.5 0.3 collective-permute-start
  14.8 2.8 %constant_dynamic-slice_fusion = (bf16[256,1024]{1,0:T(8,128)(2,1)}, bf16[256,1024]{1,0:T(8,128)(2,1)S(1)}, bf16[256,1024]{1,0:T(8,128)(2,1)S(1)}, bf16[256,1024]{1,0:T(8,128)(2,1)}) fusion(bf16[256,4096]{1,0:T(8,128)(2,1)} %param.15, s32[]{:T(128)S(6)} %select_n.54, s32[]{:T(128)S(6)} %select_n.52, s32[]{:T(128)S(6)} %select_n.51, s32[]{:T(128)S(6)} %select_n.53), kind=kLoop, calls=%fused_computation.31 | loop fusion | bytes 4194320 | tf_op jit(solution)/shard_map/dynamic_slice | solution.py:430
  17.6 0.1 collective-permute-done.2.refs_3_
  17.7 2.7 %collective-permute-done.4.refs_5_ = bf16[256,256]{1,0:T(8,128)(2,1)S(1)} collective-permute-done((bf16[256,256]{1,0:T(8,128)(2,1)S(1)}, bf16[256,256]{1,0:T(8,128)(2,1)S(1)}, u32[]{:S(2)}, u32[]{:S(2)}) %collective-permute-start.4) | collective-permute-done | bytes 131104 | tf_op jit(solution)/shard_map/ppermute | solution.py:426
  20.4 0.6 copy-done.7
  21.1 1.4 collective-permute-start.11
  22.5 1.9 collective-permute-start.12
  24.5 2.1 collective-permute-start.9
  26.6 3.5 %attention.1 = (bf16[256,768]{1,0:T(8,128)(2,1)S(1)}, bf16[256,768]{1,0:T(8,128)(2,1)S(1)}) custom-call(s32[1]{0:T(128)} %bitcast.1.ctx_ref, bf16[256,256]{1,0:T(8,128)(2,1)} %get-tuple-element.31.refs_0_, bf16[256,256]{1,0:T(8,128)(2,1)} %copy-done.8, bf16[256,256]{1,0:T(8,128)(2,1)} %copy-done.4, bf16[256,256]{1,0:T(8,128)(2,1)} %copy-done.6, ...), custom_call_target="tpu_custom_call" | custom-call | flops 110000000 | bytes 1048576 | tf_op jit(solution)/shard_map/attention/pallas_call | solution.py:100
  30.2 5.1 %collective-permute-done.11.refs_6_ = bf16[256,1024]{1,0:T(8,128)(2,1)S(1)} collective-permute-done((bf16[256,1024]{1,0:T(8,128)(2,1)S(1)}, bf16[256,1024]{1,0:T(8,128)(2,1)S(1)}, u32[]{:S(2)}, u32[]{:S(2)}) %collective-permute-start.11) | collective-permute-done | bytes 524320 | tf_op jit(solution)/shard_map/ppermute | solution.py:445
  35.3 2.3 %collective-permute-start.5 = (bf16[256,768]{1,0:T(8,128)(2,1)S(1)}, bf16[256,768]{1,0:T(8,128)(2,1)S(1)}, u32[]{:S(2)}, u32[]{:S(2)}) collective-permute-start(bf16[256,768]{1,0:T(8,128)(2,1)S(1)} %get-tuple-element.13.own0_ref), channel_id=1, source_target_pairs={{0,1},{1,0},{2,3},{3,2},{4,5},{5,4},{6,7},{7,6},{8,9},{9,8},{10,11... | collective-permute-start | bytes 1179656 | tf_op jit(solution)/shard_map/ppermute | solution.py:450
  37.6 9.7 %collective-permute-done.12.refs_7_ = bf16[256,1024]{1,0:T(8,128)(2,1)} collective-permute-done((bf16[256,1024]{1,0:T(8,128)(2,1)}, bf16[256,1024]{1,0:T(8,128)(2,1)}, u32[]{:S(2)}, u32[]{:S(2)}) %collective-permute-start.12) | collective-permute-done | bytes 524320 | tf_op jit(solution)/shard_map/ppermute | solution.py:445
  47.3 2.1 collective-permute-done.9.refs_3_
  49.4 5.5 %project.1 = bf16[16,2,16,2048]{3,2,1,0:T(8,128)(2,1)} custom-call(s32[1]{0:T(128)} %bitcast.core_ref, bf16[256,768]{1,0:T(8,128)(2,1)S(1)} %get-tuple-element.13.own0_ref, bf16[256,768]{1,0:T(8,128)(2,1)S(1)} %get-tuple-element.14.own1_ref, bf16[256,768]{1,0:T(8,128)(2,1)S(1)} %collective-permute-done.5.other0_ref, ...), custom_call_target="tpu_custom_call" | custom-call | flops 110000000 | bytes 1048576 | tf_op jit(solution)/shard_map/project/pallas_call | solution.py:160
  54.9 6.1 %all-to-all-start.1 = ((bf16[16,2,16,2048]{3,2,1,0:T(8,128)(2,1)}), bf16[16,2,16,2048]{3,2,1,0:T(8,128)(2,1)S(1)}, u32[]{:S(2)}, u32[]{:S(2)}) async-start(bf16[16,2,16,2048]{3,2,1,0:T(8,128)(2,1)} %project.1), calls=%async_computation.1 | async-start | bytes 4194304 | tf_op jit(solution)/shard_map/all_to_all | solution.py:452
  61.1 0.1 eq.84
  61.3 0.1 eq.80
  61.4 0.1 copy.31
  61.5 0.2 fusion.5
  61.8 0.2 fusion.4
  62.0 0.1 reduce_sum.32
  62.1 0.6 broadcast_multiply_fusion
  62.9 0.1 copy.34
  63.1 0.7 fusion.1
  63.8 0.3 copy.37
  64.1 0.7 fusion
  64.8 0.9 copy.36
  65.7 0.5 reshape.81
  66.2 0.3 copy.27
  66.5 1.1 add_convert_fusion.dispatch_ref
  67.6 22.0 %all-to-all-done.1 = bf16[16,2,16,2048]{3,2,1,0:T(8,128)(2,1)S(1)} async-done(((bf16[16,2,16,2048]{3,2,1,0:T(8,128)(2,1)}), bf16[16,2,16,2048]{3,2,1,0:T(8,128)(2,1)S(1)}, u32[]{:S(2)}, u32[]{:S(2)}) %all-to-all-start.1) | async-done | bytes 2097184 | tf_op jit(solution)/shard_map/all_to_all | solution.py:452
  89.6 2.2 norm_dispatch.1
  91.8 60.9 %all_to_all.20 = bf16[128,8,2048]{2,1,0:T(8,128)(2,1)S(1)} all-to-all(bf16[128,8,2048]{2,1,0:T(8,128)(2,1)S(1)} %bitcast.45), channel_id=1, replica_groups=mesh['x'=4,'zl'=2,'zh'=2,'yh'=2,'yl'=2,'core'=2] {'x','zl','zh','yh','yl..., dimensions={0} | all-to-all | bytes 8388608 | tf_op jit(solution)/shard_map/all_to_all | solution.py:463
  152.8 15.0 %experts.1 = bf16[1024,2048]{1,0:T(8,128)(2,1)} custom-call(bf16[1024,2048]{1,0:T(8,128)(2,1)S(1)} %bitcast.46, bf16[4096,768]{1,0:T(8,128)(2,1)} %bitcast.56, bf16[4096,768]{1,0:T(8,128)(2,1)} %bitcast.57, bf16[768,4096]{1,0:T(8,128)(2,1)} %bitcast.58), custom_call_target="tpu_custom_call" | custom-call | flops 15399999488 | bytes 1048576 | tf_op jit(solution)/shard_map/experts/pallas_call | solution.py:334
  167.8 5.6 %all-to-all-start.3 = ((bf16[128,8,2048]{2,1,0:T(8,128)(2,1)}), bf16[128,8,2048]{2,1,0:T(8,128)(2,1)}, u32[]{:S(2)}, u32[]{:S(2)}) async-start(bf16[128,8,2048]{2,1,0:T(8,128)(2,1)} %bitcast.50), calls=%async_computation.3 | async-start | bytes 8388608 | tf_op jit(solution)/shard_map/all_to_all | solution.py:469
  173.8 0.1 copy.42
  174.0 1.6 select_reduce_fusion.1
  175.7 50.3 %all-to-all-done.3 = bf16[128,8,2048]{2,1,0:T(8,128)(2,1)} async-done(((bf16[128,8,2048]{2,1,0:T(8,128)(2,1)}), bf16[128,8,2048]{2,1,0:T(8,128)(2,1)}, u32[]{:S(2)}, u32[]{:S(2)}) %all-to-all-start.3) | async-done | bytes 4194336 | tf_op jit(solution)/shard_map/all_to_all | solution.py:469
  226.1 3.2 %combine.1 = bf16[64,4096]{1,0:T(8,128)(2,1)S(1)} custom-call(bf16[1024,2048]{1,0:T(8,128)(2,1)} %bitcast.22.ret_ref, bf16[256,1024]{1,0:T(8,128)(2,1)S(1)} %pad_maximum_fusion.1.combine_ref, bf16[2,64,2048]{2,1,0:T(8,128)(2,1)S(1)} %get-tuple-element.20.stream_ref), custom_call_target="tpu_custom_call" | custom-call | flops 4400000000 | bytes 1048576 | tf_op jit(solution)/shard_map/combine/pallas_call | solution.py:243
  229.2 1.0 reshape.89
  (59 shorter events, 1.0 us)
Async XLA Ops:
  0.0 8.4 %copy-start.1 = (bf16[4,256,256]{2,1,0:T(8,128)(2,1)S(1)}, bf16[4,256,256]{2,1,0:T(8,128)(2,1)}, u32[]{:S(2)}) copy-start(bf16[4,256,256]{2,1,0:T(8,128)(2,1)} %param.11) | copy-start | bytes 1572868
  2.2 24.4 %all-to-all-start = ((bf16[8,256,256]{2,1,0:T(8,128)(2,1)}), bf16[8,256,256]{2,1,0:T(8,128)(2,1)S(1)}, u32[]{:S(2)}, u32[]{:S(2)}) async-start(bf16[8,256,256]{2,1,0:T(8,128)(2,1)} %broadcast_in_dim.38), calls=%async_computation | async-start | bytes 2097152 | tf_op jit(solution)/shard_map/all_to_all | solution.py:448
  9.1 8.5 %collective-permute-start.1 = (bf16[256,256]{1,0:T(8,128)(2,1)S(1)}, bf16[256,256]{1,0:T(8,128)(2,1)S(1)}, u32[]{:S(2)}, u32[]{:S(2)}) collective-permute-start(bf16[256,256]{1,0:T(8,128)(2,1)S(1)} %get-tuple-element.32), channel_id=1, source_target_pairs={{0,2},{1,3},{2,0},{3,1},{4,6},{5,7},{6,4},{7,5},{8,10},{9,11},{10,... | collective-permute-start | bytes 393224 | tf_op jit(solution)/shard_map/ppermute | solution.py:426
  10.4 7.3 %collective-permute-start.3 = (bf16[256,256]{1,0:T(8,128)(2,1)S(1)}, bf16[256,256]{1,0:T(8,128)(2,1)S(1)}, u32[]{:S(2)}, u32[]{:S(2)}) collective-permute-start(bf16[256,256]{1,0:T(8,128)(2,1)S(1)} %get-tuple-element.32), channel_id=1, source_target_pairs={{0,6},{1,7},{2,4},{3,5},{4,2},{5,3},{6,0},{7,1},{8,14},{9,15},{10,... | collective-permute-start | bytes 393224 | tf_op jit(solution)/shard_map/ppermute | solution.py:426
  12.3 5.4 %collective-permute-start.2 = (bf16[256,256]{1,0:T(8,128)(2,1)S(1)}, bf16[256,256]{1,0:T(8,128)(2,1)S(1)}, u32[]{:S(2)}, u32[]{:S(2)}) collective-permute-start(bf16[256,256]{1,0:T(8,128)(2,1)S(1)} %get-tuple-element.29), channel_id=1, source_target_pairs={{0,3},{1,2},{2,1},{3,0},{4,7},{5,6},{6,5},{7,4},{8,11},{9,10},{10,... | collective-permute-start | bytes 393224 | tf_op jit(solution)/shard_map/ppermute | solution.py:426
  14.1 6.3 %collective-permute-start.4 = (bf16[256,256]{1,0:T(8,128)(2,1)S(1)}, bf16[256,256]{1,0:T(8,128)(2,1)S(1)}, u32[]{:S(2)}, u32[]{:S(2)}) collective-permute-start(bf16[256,256]{1,0:T(8,128)(2,1)S(1)} %get-tuple-element.29), channel_id=1, source_target_pairs={{0,7},{1,6},{2,5},{3,4},{4,3},{5,2},{6,1},{7,0},{8,15},{9,14},{10,... | collective-permute-start | bytes 393224 | tf_op jit(solution)/shard_map/ppermute | solution.py:426
  14.5 3.1 %collective-permute-start = (bf16[256,256]{1,0:T(8,128)(2,1)S(1)}, bf16[256,256]{1,0:T(8,128)(2,1)S(1)}, u32[]{:S(2)}, u32[]{:S(2)}) collective-permute-start(bf16[256,256]{1,0:T(8,128)(2,1)S(1)} %get-tuple-element.30), channel_id=1, source_target_pairs={{0,1},{1,0},{2,3},{3,2},{4,5},{5,4},{6,7},{7,6},{8,9},{9,8},{10,11... | collective-permute-start | bytes 393224 | tf_op jit(solution)/shard_map/ppermute | solution.py:426
  17.6 2.9 %copy-start.8 = (bf16[256,256]{1,0:T(8,128)(2,1)}, bf16[256,256]{1,0:T(8,128)(2,1)S(1)}, u32[]{:S(2)}) copy-start(bf16[256,256]{1,0:T(8,128)(2,1)S(1)} %collective-permute-done.refs_1_) | copy-start | bytes 393220
  17.6 9.0 %copy-start.4 = (bf16[256,256]{1,0:T(8,128)(2,1)}, bf16[256,256]{1,0:T(8,128)(2,1)S(1)}, u32[]{:S(2)}) copy-start(bf16[256,256]{1,0:T(8,128)(2,1)S(1)} %collective-permute-done.1.refs_2_) | copy-start | bytes 393220
  17.7 8.9 %copy-start.6 = (bf16[256,256]{1,0:T(8,128)(2,1)}, bf16[256,256]{1,0:T(8,128)(2,1)S(1)}, u32[]{:S(2)}) copy-start(bf16[256,256]{1,0:T(8,128)(2,1)S(1)} %collective-permute-done.2.refs_3_) | copy-start | bytes 393220
  17.7 8.9 %copy-start.5 = (bf16[256,256]{1,0:T(8,128)(2,1)}, bf16[256,256]{1,0:T(8,128)(2,1)S(1)}, u32[]{:S(2)}) copy-start(bf16[256,256]{1,0:T(8,128)(2,1)S(1)} %collective-permute-done.3.refs_4_) | copy-start | bytes 393220
  20.4 0.7 copy-start.7
  21.1 3.4 %collective-permute-start.10 = (bf16[256,1024]{1,0:T(8,128)(2,1)}, bf16[256,1024]{1,0:T(8,128)(2,1)S(1)}, u32[]{:S(2)}, u32[]{:S(2)}) collective-permute-start(bf16[256,1024]{1,0:T(8,128)(2,1)} %get-tuple-element.18), channel_id=1, source_target_pairs={{0,1},{1,0},{2,3},{3,2},{4,5},{5,4},{6,7},{7,6},{8,9},{9,8},{10,11... | collective-permute-start | bytes 1572872 | tf_op jit(solution)/shard_map/ppermute | solution.py:445
  21.1 14.2 %collective-permute-start.11 = (bf16[256,1024]{1,0:T(8,128)(2,1)S(1)}, bf16[256,1024]{1,0:T(8,128)(2,1)S(1)}, u32[]{:S(2)}, u32[]{:S(2)}) collective-permute-start(bf16[256,1024]{1,0:T(8,128)(2,1)S(1)} %get-tuple-element.17.refs_4_), channel_id=1, source_target_pairs={{0,6},{1,7},{2,4},{3,5},{4,2},{5,3},{6,0},{7,1},{8,14},{9,15},{10,... | collective-permute-start | bytes 1572872 | tf_op jit(solution)/shard_map/ppermute | solution.py:445
  22.5 24.8 %collective-permute-start.12 = (bf16[256,1024]{1,0:T(8,128)(2,1)}, bf16[256,1024]{1,0:T(8,128)(2,1)}, u32[]{:S(2)}, u32[]{:S(2)}) collective-permute-start(bf16[256,1024]{1,0:T(8,128)(2,1)} %get-tuple-element.18), channel_id=1, source_target_pairs={{0,7},{1,6},{2,5},{3,4},{4,3},{5,2},{6,1},{7,0},{8,15},{9,14},{10,... | collective-permute-start | bytes 1572872 | tf_op jit(solution)/shard_map/ppermute | solution.py:445
  24.4 22.9 %collective-permute-start.7 = (bf16[256,1024]{1,0:T(8,128)(2,1)}, bf16[256,1024]{1,0:T(8,128)(2,1)}, u32[]{:S(2)}, u32[]{:S(2)}) collective-permute-start(bf16[256,1024]{1,0:T(8,128)(2,1)} %get-tuple-element.16), channel_id=1, source_target_pairs={{0,1},{1,0},{2,3},{3,2},{4,5},{5,4},{6,7},{7,6},{8,9},{9,8},{10,11... | collective-permute-start | bytes 1572872 | tf_op jit(solution)/shard_map/ppermute | solution.py:442
  24.5 22.9 %collective-permute-start.8 = (bf16[256,1024]{1,0:T(8,128)(2,1)S(1)}, bf16[256,1024]{1,0:T(8,128)(2,1)}, u32[]{:S(2)}, u32[]{:S(2)}) collective-permute-start(bf16[256,1024]{1,0:T(8,128)(2,1)S(1)} %get-tuple-element.15.refs_0_), channel_id=1, source_target_pairs={{0,2},{1,3},{2,0},{3,1},{4,6},{5,7},{6,4},{7,5},{8,10},{9,11},{10,... | collective-permute-start | bytes 1572872 | tf_op jit(solution)/shard_map/ppermute | solution.py:442
  24.5 25.0 %collective-permute-start.9 = (bf16[256,1024]{1,0:T(8,128)(2,1)}, bf16[256,1024]{1,0:T(8,128)(2,1)}, u32[]{:S(2)}, u32[]{:S(2)}) collective-permute-start(bf16[256,1024]{1,0:T(8,128)(2,1)} %get-tuple-element.16), channel_id=1, source_target_pairs={{0,3},{1,2},{2,1},{3,0},{4,7},{5,6},{6,5},{7,4},{8,11},{9,10},{10,... | collective-permute-start | bytes 1572872 | tf_op jit(solution)/shard_map/ppermute | solution.py:442
  35.3 14.2 %collective-permute-start.5 = (bf16[256,768]{1,0:T(8,128)(2,1)S(1)}, bf16[256,768]{1,0:T(8,128)(2,1)S(1)}, u32[]{:S(2)}, u32[]{:S(2)}) collective-permute-start(bf16[256,768]{1,0:T(8,128)(2,1)S(1)} %get-tuple-element.13.own0_ref), channel_id=1, source_target_pairs={{0,1},{1,0},{2,3},{3,2},{4,5},{5,4},{6,7},{7,6},{8,9},{9,8},{10,11... | collective-permute-start | bytes 1179656 | tf_op jit(solution)/shard_map/ppermute | solution.py:450
  47.3 2.1 collective-permute-start.6
  54.9 6.1 %copy-start.11 = (s32[16,4,8]{0,2,1:T(8,128)S(1)}, s32[16,4,8]{0,2,1:T(8,128)}, u32[]{:S(2)}) copy-start(s32[16,4,8]{0,2,1:T(8,128)} %param.17) | copy-start | bytes 6148
  54.9 34.7 %all-to-all-start.1 = ((bf16[16,2,16,2048]{3,2,1,0:T(8,128)(2,1)}), bf16[16,2,16,2048]{3,2,1,0:T(8,128)(2,1)S(1)}, u32[]{:S(2)}, u32[]{:S(2)}) async-start(bf16[16,2,16,2048]{3,2,1,0:T(8,128)(2,1)} %project.1), calls=%async_computation.1 | async-start | bytes 4194304 | tf_op jit(solution)/shard_map/all_to_all | solution.py:452
  61.1 4.6 %copy-start.2 = (bf16[16,4,4096]{2,1,0:T(4,128)(2,1)S(1)}, bf16[16,4,4096]{2,1,0:T(4,128)(2,1)}, u32[]{:S(2)}) copy-start(bf16[16,4,4096]{2,1,0:T(4,128)(2,1)} %param.14) | copy-start | bytes 1572868
  61.8 27.9 %copy-start = (f32[4096]{0:T(1024)S(1)}, f32[4096]{0:T(1024)}, u32[]{:S(2)}) copy-start(f32[4096]{0:T(1024)} %param.16) | copy-start | bytes 49156
  62.0 2.8 %copy-start.9 = (s32[512]{0:T(512)}, s32[512]{0:T(512)S(1)}, u32[]{:S(2)}) copy-start(s32[512]{0:T(512)S(1)} %fusion.4) | copy-start | bytes 6148
  167.8 5.7 %copy-start.10 = (s32[512]{0:T(512)S(1)}, s32[512]{0:T(512)}, u32[]{:S(2)}) copy-start(s32[512]{0:T(512)} %copy-done.9) | copy-start | bytes 6148
  167.8 5.8 %copy-start.3 = (s32[16,4,8]{2,1,0:T(4,128)S(1)}, s32[16,4,8]{2,1,0:T(4,128)}, u32[]{:S(2)}) copy-start(s32[16,4,8]{2,1,0:T(4,128)} %get-tuple-element.33) | copy-start | bytes 6148
  167.8 6.1 %copy-start.12 = (f32[16,4,8]{0,2,1:T(8,128)S(1)}, f32[16,4,8]{0,2,1:T(8,128)}, u32[]{:S(2)}) copy-start(f32[16,4,8]{0,2,1:T(8,128)} %param.18) | copy-start | bytes 6148
  167.8 58.2 %all-to-all-start.3 = ((bf16[128,8,2048]{2,1,0:T(8,128)(2,1)}), bf16[128,8,2048]{2,1,0:T(8,128)(2,1)}, u32[]{:S(2)}, u32[]{:S(2)}) async-start(bf16[128,8,2048]{2,1,0:T(8,128)(2,1)} %bitcast.50), calls=%async_computation.3 | async-start | bytes 8388608 | tf_op jit(solution)/shard_map/all_to_all | solution.py:469

commit v4 on v3

--- a/solution.py
+++ b/solution.py
@@ -152,7 +152,7 @@
 
 def project(core, own, other, first, second):
     rows, width = own[0].shape[0], first[0].shape[1]
-    tile = 512
+    tile = 1024
     steps = 2 * width // tile
     att = pl.BlockSpec(own[0].shape, lambda i: (0, 0))
     in_first = pl.BlockSpec((256, tile), lambda i: (0, jnp.minimum(i, steps // 2 - 1)))

time: 231 us -> 230 us (level)
  no operation moved by 1% of the time
where the time goes in v4:
time: 230 us
  waiting for transfers between devices  92.1 us (40%)
  blocking collectives  60.9 us (26%)
  starting transfers between devices  31.5 us (14%)
  Pallas kernels  29 us (13%)
  local copies, waits for them, and re-layouts  10.6 us (5%)
  other arithmetic  5.36 us (2%)
    all_to_all x1, blocking collectives, local(): lax.all_to_all(outgoing.reshape(experts_all, 2 * capacity, half), ALL, 0,...  60.9 us
    all_to_all x1, waiting for transfers between devices, local(): lax.all_to_all(produced.reshape(experts_all, 2 * capacity, half), ALL, 0,...  50.3 us
    all_to_all x1, waiting for transfers between devices, local(): parts = lax.all_to_all(partial_sums, EXP, 0, 0, tiled=True)  22 us
    ppermute x6, waiting for transfers between devices, local(): lax.ppermute(w, ring, pairs[m])  17 us
    pallas_call x1, Pallas kernels, experts(): pl.pallas_call(expert_kernel, out_shape=pltpu.HBM((rows, width), BF16), i...  15 us
    all_to_all x1, starting transfers between devices, local(): kv = lax.all_to_all(kv_send, CTX, 0, 0, tiled=True)  6.2 us
    all_to_all x1, starting transfers between devices, local(): parts = lax.all_to_all(partial_sums, EXP, 0, 0, tiled=True)  6.14 us
    ppermute x5, starting transfers between devices, local(): chunks.append(lax.ppermute(chunk, ring, pairs[m]))  5.72 us
  transfers between devices with their start and end apart: 16, of which 7 were waited for; matrix products, arithmetic and copies ran while one was open for 5% of the time, Pallas kernels for 2%

profile of v4, /device:TPU:1, one launch (start us, length us, event | category | flops | bytes accessed | tf_op | source)
XLA Modules:
  0.0 229.8 jit_solution(7281379930291019942)
XLA Ops:
  0.0 1.1 dynamic-slice_bitcast_fusion.4
  1.2 1.0 broadcast_in_dim.38
  2.2 6.2 %all-to-all-start = ((bf16[8,256,256]{2,1,0:T(8,128)(2,1)}), bf16[8,256,256]{2,1,0:T(8,128)(2,1)S(1)}, u32[]{:S(2)}, u32[]{:S(2)}) async-start(bf16[8,256,256]{2,1,0:T(8,128)(2,1)} %broadcast_in_dim.38), calls=%async_computation | async-start | bytes 2097152 | tf_op jit(solution)/shard_map/all_to_all | solution.py:448
  8.4 0.7 dynamic-slice_bitcast_fusion
  9.1 1.3 collective-permute-start.1
  10.4 1.9 collective-permute-start.3
  12.3 1.8 collective-permute-start.2
  14.1 0.4 collective-permute-start.4
  14.5 0.3 collective-permute-start
  14.8 2.8 %constant_dynamic-slice_fusion = (bf16[256,1024]{1,0:T(8,128)(2,1)}, bf16[256,1024]{1,0:T(8,128)(2,1)S(1)}, bf16[256,1024]{1,0:T(8,128)(2,1)S(1)}, bf16[256,1024]{1,0:T(8,128)(2,1)}) fusion(bf16[256,4096]{1,0:T(8,128)(2,1)} %param.15, s32[]{:T(128)S(6)} %select_n.54, s32[]{:T(128)S(6)} %select_n.52, s32[]{:T(128)S(6)} %select_n.51, s32[]{:T(128)S(6)} %select_n.53), kind=kLoop, calls=%fused_computation.31 | loop fusion | bytes 4194320 | tf_op jit(solution)/shard_map/dynamic_slice | solution.py:430
  17.6 0.1 collective-permute-done.2.refs_3_
  17.7 2.7 %collective-permute-done.4.refs_5_ = bf16[256,256]{1,0:T(8,128)(2,1)S(1)} collective-permute-done((bf16[256,256]{1,0:T(8,128)(2,1)S(1)}, bf16[256,256]{1,0:T(8,128)(2,1)S(1)}, u32[]{:S(2)}, u32[]{:S(2)}) %collective-permute-start.4) | collective-permute-done | bytes 131104 | tf_op jit(solution)/shard_map/ppermute | solution.py:426
  20.4 0.6 copy-done.7
  21.1 1.4 collective-permute-start.11
  22.5 1.9 collective-permute-start.12
  24.5 2.1 collective-permute-start.9
  26.6 3.5 %attention.1 = (bf16[256,768]{1,0:T(8,128)(2,1)S(1)}, bf16[256,768]{1,0:T(8,128)(2,1)S(1)}) custom-call(s32[1]{0:T(128)} %bitcast.1.ctx_ref, bf16[256,256]{1,0:T(8,128)(2,1)} %get-tuple-element.31.refs_0_, bf16[256,256]{1,0:T(8,128)(2,1)} %copy-done.8, bf16[256,256]{1,0:T(8,128)(2,1)} %copy-done.4, bf16[256,256]{1,0:T(8,128)(2,1)} %copy-done.6, ...), custom_call_target="tpu_custom_call" | custom-call | flops 110000000 | bytes 1048576 | tf_op jit(solution)/shard_map/attention/pallas_call | solution.py:100
  30.2 5.1 %collective-permute-done.11.refs_6_ = bf16[256,1024]{1,0:T(8,128)(2,1)S(1)} collective-permute-done((bf16[256,1024]{1,0:T(8,128)(2,1)S(1)}, bf16[256,1024]{1,0:T(8,128)(2,1)S(1)}, u32[]{:S(2)}, u32[]{:S(2)}) %collective-permute-start.11) | collective-permute-done | bytes 524320 | tf_op jit(solution)/shard_map/ppermute | solution.py:445
  35.3 2.3 %collective-permute-start.5 = (bf16[256,768]{1,0:T(8,128)(2,1)S(1)}, bf16[256,768]{1,0:T(8,128)(2,1)S(1)}, u32[]{:S(2)}, u32[]{:S(2)}) collective-permute-start(bf16[256,768]{1,0:T(8,128)(2,1)S(1)} %get-tuple-element.13.own0_ref), channel_id=1, source_target_pairs={{0,1},{1,0},{2,3},{3,2},{4,5},{5,4},{6,7},{7,6},{8,9},{9,8},{10,11... | collective-permute-start | bytes 1179656 | tf_op jit(solution)/shard_map/ppermute | solution.py:450
  37.6 9.7 %collective-permute-done.12.refs_7_ = bf16[256,1024]{1,0:T(8,128)(2,1)} collective-permute-done((bf16[256,1024]{1,0:T(8,128)(2,1)}, bf16[256,1024]{1,0:T(8,128)(2,1)}, u32[]{:S(2)}, u32[]{:S(2)}) %collective-permute-start.12) | collective-permute-done | bytes 524320 | tf_op jit(solution)/shard_map/ppermute | solution.py:445
  47.3 2.1 collective-permute-done.9.refs_3_
  49.4 5.1 %project.1 = bf16[16,2,16,2048]{3,2,1,0:T(8,128)(2,1)} custom-call(s32[1]{0:T(128)} %bitcast.core_ref, bf16[256,768]{1,0:T(8,128)(2,1)S(1)} %get-tuple-element.13.own0_ref, bf16[256,768]{1,0:T(8,128)(2,1)S(1)} %get-tuple-element.14.own1_ref, bf16[256,768]{1,0:T(8,128)(2,1)S(1)} %collective-permute-done.5.other0_ref, ...), custom_call_target="tpu_custom_call" | custom-call | flops 110000000 | bytes 1048576 | tf_op jit(solution)/shard_map/project/pallas_call | solution.py:160
  54.5 6.1 %all-to-all-start.1 = ((bf16[16,2,16,2048]{3,2,1,0:T(8,128)(2,1)}), bf16[16,2,16,2048]{3,2,1,0:T(8,128)(2,1)S(1)}, u32[]{:S(2)}, u32[]{:S(2)}) async-start(bf16[16,2,16,2048]{3,2,1,0:T(8,128)(2,1)} %project.1), calls=%async_computation.1 | async-start | bytes 4194304 | tf_op jit(solution)/shard_map/all_to_all | solution.py:452
  60.8 0.1 eq.84
  60.9 0.1 eq.80
  61.0 0.1 copy.31
  61.1 0.2 fusion.5
  61.4 0.2 fusion.4
  61.7 0.1 reduce_sum.32
  61.8 0.6 broadcast_multiply_fusion
  62.5 0.1 copy.34
  62.7 0.7 fusion.1
  63.4 0.3 copy.37
  63.7 0.7 fusion
  64.4 0.9 copy.36
  65.3 0.5 reshape.81
  65.8 0.3 copy.27
  66.1 1.1 add_convert_fusion.dispatch_ref
  67.3 22.0 %all-to-all-done.1 = bf16[16,2,16,2048]{3,2,1,0:T(8,128)(2,1)S(1)} async-done(((bf16[16,2,16,2048]{3,2,1,0:T(8,128)(2,1)}), bf16[16,2,16,2048]{3,2,1,0:T(8,128)(2,1)S(1)}, u32[]{:S(2)}, u32[]{:S(2)}) %all-to-all-start.1) | async-done | bytes 2097184 | tf_op jit(solution)/shard_map/all_to_all | solution.py:452
  89.3 2.2 norm_dispatch.1
  91.5 60.9 %all_to_all.20 = bf16[128,8,2048]{2,1,0:T(8,128)(2,1)S(1)} all-to-all(bf16[128,8,2048]{2,1,0:T(8,128)(2,1)S(1)} %bitcast.45), channel_id=1, replica_groups=mesh['x'=4,'zl'=2,'zh'=2,'yh'=2,'yl'=2,'core'=2] {'x','zl','zh','yh','yl..., dimensions={0} | all-to-all | bytes 8388608 | tf_op jit(solution)/shard_map/all_to_all | solution.py:463
  152.4 15.0 %experts.1 = bf16[1024,2048]{1,0:T(8,128)(2,1)} custom-call(bf16[1024,2048]{1,0:T(8,128)(2,1)S(1)} %bitcast.46, bf16[4096,768]{1,0:T(8,128)(2,1)} %bitcast.56, bf16[4096,768]{1,0:T(8,128)(2,1)} %bitcast.57, bf16[768,4096]{1,0:T(8,128)(2,1)} %bitcast.58), custom_call_target="tpu_custom_call" | custom-call | flops 15399999488 | bytes 1048576 | tf_op jit(solution)/shard_map/experts/pallas_call | solution.py:334
  167.4 5.6 %all-to-all-start.3 = ((bf16[128,8,2048]{2,1,0:T(8,128)(2,1)}), bf16[128,8,2048]{2,1,0:T(8,128)(2,1)}, u32[]{:S(2)}, u32[]{:S(2)}) async-start(bf16[128,8,2048]{2,1,0:T(8,128)(2,1)} %bitcast.50), calls=%async_computation.3 | async-start | bytes 8388608 | tf_op jit(solution)/shard_map/all_to_all | solution.py:469
  173.4 0.1 copy.42
  173.6 1.6 select_reduce_fusion.1
  175.3 50.3 %all-to-all-done.3 = bf16[128,8,2048]{2,1,0:T(8,128)(2,1)} async-done(((bf16[128,8,2048]{2,1,0:T(8,128)(2,1)}), bf16[128,8,2048]{2,1,0:T(8,128)(2,1)}, u32[]{:S(2)}, u32[]{:S(2)}) %all-to-all-start.3) | async-done | bytes 4194336 | tf_op jit(solution)/shard_map/all_to_all | solution.py:469
  225.7 3.2 %combine.1 = bf16[64,4096]{1,0:T(8,128)(2,1)S(1)} custom-call(bf16[1024,2048]{1,0:T(8,128)(2,1)} %bitcast.22.ret_ref, bf16[256,1024]{1,0:T(8,128)(2,1)S(1)} %pad_maximum_fusion.1.combine_ref, bf16[2,64,2048]{2,1,0:T(8,128)(2,1)S(1)} %get-tuple-element.20.stream_ref), custom_call_target="tpu_custom_call" | custom-call | flops 4400000000 | bytes 1048576 | tf_op jit(solution)/shard_map/combine/pallas_call | solution.py:243
  228.9 1.0 reshape.89
  (59 shorter events, 1.0 us)
Async XLA Ops:
  0.0 8.4 %copy-start.1 = (bf16[4,256,256]{2,1,0:T(8,128)(2,1)S(1)}, bf16[4,256,256]{2,1,0:T(8,128)(2,1)}, u32[]{:S(2)}) copy-start(bf16[4,256,256]{2,1,0:T(8,128)(2,1)} %param.11) | copy-start | bytes 1572868
  2.2 24.4 %all-to-all-start = ((bf16[8,256,256]{2,1,0:T(8,128)(2,1)}), bf16[8,256,256]{2,1,0:T(8,128)(2,1)S(1)}, u32[]{:S(2)}, u32[]{:S(2)}) async-start(bf16[8,256,256]{2,1,0:T(8,128)(2,1)} %broadcast_in_dim.38), calls=%async_computation | async-start | bytes 2097152 | tf_op jit(solution)/shard_map/all_to_all | solution.py:448
  9.1 8.5 %collective-permute-start.1 = (bf16[256,256]{1,0:T(8,128)(2,1)S(1)}, bf16[256,256]{1,0:T(8,128)(2,1)S(1)}, u32[]{:S(2)}, u32[]{:S(2)}) collective-permute-start(bf16[256,256]{1,0:T(8,128)(2,1)S(1)} %get-tuple-element.32), channel_id=1, source_target_pairs={{0,2},{1,3},{2,0},{3,1},{4,6},{5,7},{6,4},{7,5},{8,10},{9,11},{10,... | collective-permute-start | bytes 393224 | tf_op jit(solution)/shard_map/ppermute | solution.py:426
  10.4 7.3 %collective-permute-start.3 = (bf16[256,256]{1,0:T(8,128)(2,1)S(1)}, bf16[256,256]{1,0:T(8,128)(2,1)S(1)}, u32[]{:S(2)}, u32[]{:S(2)}) collective-permute-start(bf16[256,256]{1,0:T(8,128)(2,1)S(1)} %get-tuple-element.32), channel_id=1, source_target_pairs={{0,6},{1,7},{2,4},{3,5},{4,2},{5,3},{6,0},{7,1},{8,14},{9,15},{10,... | collective-permute-start | bytes 393224 | tf_op jit(solution)/shard_map/ppermute | solution.py:426
  12.3 5.4 %collective-permute-start.2 = (bf16[256,256]{1,0:T(8,128)(2,1)S(1)}, bf16[256,256]{1,0:T(8,128)(2,1)S(1)}, u32[]{:S(2)}, u32[]{:S(2)}) collective-permute-start(bf16[256,256]{1,0:T(8,128)(2,1)S(1)} %get-tuple-element.29), channel_id=1, source_target_pairs={{0,3},{1,2},{2,1},{3,0},{4,7},{5,6},{6,5},{7,4},{8,11},{9,10},{10,... | collective-permute-start | bytes 393224 | tf_op jit(solution)/shard_map/ppermute | solution.py:426
  14.1 6.3 %collective-permute-start.4 = (bf16[256,256]{1,0:T(8,128)(2,1)S(1)}, bf16[256,256]{1,0:T(8,128)(2,1)S(1)}, u32[]{:S(2)}, u32[]{:S(2)}) collective-permute-start(bf16[256,256]{1,0:T(8,128)(2,1)S(1)} %get-tuple-element.29), channel_id=1, source_target_pairs={{0,7},{1,6},{2,5},{3,4},{4,3},{5,2},{6,1},{7,0},{8,15},{9,14},{10,... | collective-permute-start | bytes 393224 | tf_op jit(solution)/shard_map/ppermute | solution.py:426
  14.5 3.1 %collective-permute-start = (bf16[256,256]{1,0:T(8,128)(2,1)S(1)}, bf16[256,256]{1,0:T(8,128)(2,1)S(1)}, u32[]{:S(2)}, u32[]{:S(2)}) collective-permute-start(bf16[256,256]{1,0:T(8,128)(2,1)S(1)} %get-tuple-element.30), channel_id=1, source_target_pairs={{0,1},{1,0},{2,3},{3,2},{4,5},{5,4},{6,7},{7,6},{8,9},{9,8},{10,11... | collective-permute-start | bytes 393224 | tf_op jit(solution)/shard_map/ppermute | solution.py:426
  17.6 2.9 %copy-start.8 = (bf16[256,256]{1,0:T(8,128)(2,1)}, bf16[256,256]{1,0:T(8,128)(2,1)S(1)}, u32[]{:S(2)}) copy-start(bf16[256,256]{1,0:T(8,128)(2,1)S(1)} %collective-permute-done.refs_1_) | copy-start | bytes 393220
  17.6 9.0 %copy-start.4 = (bf16[256,256]{1,0:T(8,128)(2,1)}, bf16[256,256]{1,0:T(8,128)(2,1)S(1)}, u32[]{:S(2)}) copy-start(bf16[256,256]{1,0:T(8,128)(2,1)S(1)} %collective-permute-done.1.refs_2_) | copy-start | bytes 393220
  17.7 8.9 %copy-start.6 = (bf16[256,256]{1,0:T(8,128)(2,1)}, bf16[256,256]{1,0:T(8,128)(2,1)S(1)}, u32[]{:S(2)}) copy-start(bf16[256,256]{1,0:T(8,128)(2,1)S(1)} %collective-permute-done.2.refs_3_) | copy-start | bytes 393220
  17.7 8.9 %copy-start.5 = (bf16[256,256]{1,0:T(8,128)(2,1)}, bf16[256,256]{1,0:T(8,128)(2,1)S(1)}, u32[]{:S(2)}) copy-start(bf16[256,256]{1,0:T(8,128)(2,1)S(1)} %collective-permute-done.3.refs_4_) | copy-start | bytes 393220
  20.4 0.7 copy-start.7
  21.1 3.4 %collective-permute-start.10 = (bf16[256,1024]{1,0:T(8,128)(2,1)}, bf16[256,1024]{1,0:T(8,128)(2,1)S(1)}, u32[]{:S(2)}, u32[]{:S(2)}) collective-permute-start(bf16[256,1024]{1,0:T(8,128)(2,1)} %get-tuple-element.18), channel_id=1, source_target_pairs={{0,1},{1,0},{2,3},{3,2},{4,5},{5,4},{6,7},{7,6},{8,9},{9,8},{10,11... | collective-permute-start | bytes 1572872 | tf_op jit(solution)/shard_map/ppermute | solution.py:445
  21.1 14.2 %collective-permute-start.11 = (bf16[256,1024]{1,0:T(8,128)(2,1)S(1)}, bf16[256,1024]{1,0:T(8,128)(2,1)S(1)}, u32[]{:S(2)}, u32[]{:S(2)}) collective-permute-start(bf16[256,1024]{1,0:T(8,128)(2,1)S(1)} %get-tuple-element.17.refs_4_), channel_id=1, source_target_pairs={{0,6},{1,7},{2,4},{3,5},{4,2},{5,3},{6,0},{7,1},{8,14},{9,15},{10,... | collective-permute-start | bytes 1572872 | tf_op jit(solution)/shard_map/ppermute | solution.py:445
  22.5 24.8 %collective-permute-start.12 = (bf16[256,1024]{1,0:T(8,128)(2,1)}, bf16[256,1024]{1,0:T(8,128)(2,1)}, u32[]{:S(2)}, u32[]{:S(2)}) collective-permute-start(bf16[256,1024]{1,0:T(8,128)(2,1)} %get-tuple-element.18), channel_id=1, source_target_pairs={{0,7},{1,6},{2,5},{3,4},{4,3},{5,2},{6,1},{7,0},{8,15},{9,14},{10,... | collective-permute-start | bytes 1572872 | tf_op jit(solution)/shard_map/ppermute | solution.py:445
  24.4 22.9 %collective-permute-start.7 = (bf16[256,1024]{1,0:T(8,128)(2,1)}, bf16[256,1024]{1,0:T(8,128)(2,1)}, u32[]{:S(2)}, u32[]{:S(2)}) collective-permute-start(bf16[256,1024]{1,0:T(8,128)(2,1)} %get-tuple-element.16), channel_id=1, source_target_pairs={{0,1},{1,0},{2,3},{3,2},{4,5},{5,4},{6,7},{7,6},{8,9},{9,8},{10,11... | collective-permute-start | bytes 1572872 | tf_op jit(solution)/shard_map/ppermute | solution.py:442
  24.5 22.9 %collective-permute-start.8 = (bf16[256,1024]{1,0:T(8,128)(2,1)S(1)}, bf16[256,1024]{1,0:T(8,128)(2,1)}, u32[]{:S(2)}, u32[]{:S(2)}) collective-permute-start(bf16[256,1024]{1,0:T(8,128)(2,1)S(1)} %get-tuple-element.15.refs_0_), channel_id=1, source_target_pairs={{0,2},{1,3},{2,0},{3,1},{4,6},{5,7},{6,4},{7,5},{8,10},{9,11},{10,... | collective-permute-start | bytes 1572872 | tf_op jit(solution)/shard_map/ppermute | solution.py:442
  24.5 25.0 %collective-permute-start.9 = (bf16[256,1024]{1,0:T(8,128)(2,1)}, bf16[256,1024]{1,0:T(8,128)(2,1)}, u32[]{:S(2)}, u32[]{:S(2)}) collective-permute-start(bf16[256,1024]{1,0:T(8,128)(2,1)} %get-tuple-element.16), channel_id=1, source_target_pairs={{0,3},{1,2},{2,1},{3,0},{4,7},{5,6},{6,5},{7,4},{8,11},{9,10},{10,... | collective-permute-start | bytes 1572872 | tf_op jit(solution)/shard_map/ppermute | solution.py:442
  35.3 14.2 %collective-permute-start.5 = (bf16[256,768]{1,0:T(8,128)(2,1)S(1)}, bf16[256,768]{1,0:T(8,128)(2,1)S(1)}, u32[]{:S(2)}, u32[]{:S(2)}) collective-permute-start(bf16[256,768]{1,0:T(8,128)(2,1)S(1)} %get-tuple-element.13.own0_ref), channel_id=1, source_target_pairs={{0,1},{1,0},{2,3},{3,2},{4,5},{5,4},{6,7},{7,6},{8,9},{9,8},{10,11... | collective-permute-start | bytes 1179656 | tf_op jit(solution)/shard_map/ppermute | solution.py:450
  47.3 2.1 collective-permute-start.6
  54.5 6.1 %copy-start.11 = (s32[16,4,8]{0,2,1:T(8,128)S(1)}, s32[16,4,8]{0,2,1:T(8,128)}, u32[]{:S(2)}) copy-start(s32[16,4,8]{0,2,1:T(8,128)} %param.17) | copy-start | bytes 6148
  54.5 34.7 %all-to-all-start.1 = ((bf16[16,2,16,2048]{3,2,1,0:T(8,128)(2,1)}), bf16[16,2,16,2048]{3,2,1,0:T(8,128)(2,1)S(1)}, u32[]{:S(2)}, u32[]{:S(2)}) async-start(bf16[16,2,16,2048]{3,2,1,0:T(8,128)(2,1)} %project.1), calls=%async_computation.1 | async-start | bytes 4194304 | tf_op jit(solution)/shard_map/all_to_all | solution.py:452
  60.7 4.6 %copy-start.2 = (bf16[16,4,4096]{2,1,0:T(4,128)(2,1)S(1)}, bf16[16,4,4096]{2,1,0:T(4,128)(2,1)}, u32[]{:S(2)}) copy-start(bf16[16,4,4096]{2,1,0:T(4,128)(2,1)} %param.14) | copy-start | bytes 1572868
  61.4 27.9 %copy-start = (f32[4096]{0:T(1024)S(1)}, f32[4096]{0:T(1024)}, u32[]{:S(2)}) copy-start(f32[4096]{0:T(1024)} %param.16) | copy-start | bytes 49156
  61.6 2.8 %copy-start.9 = (s32[512]{0:T(512)}, s32[512]{0:T(512)S(1)}, u32[]{:S(2)}) copy-start(s32[512]{0:T(512)S(1)} %fusion.4) | copy-start | bytes 6148
  167.4 5.7 %copy-start.10 = (s32[512]{0:T(512)S(1)}, s32[512]{0:T(512)}, u32[]{:S(2)}) copy-start(s32[512]{0:T(512)} %copy-done.9) | copy-start | bytes 6148
  167.4 5.8 %copy-start.3 = (s32[16,4,8]{2,1,0:T(4,128)S(1)}, s32[16,4,8]{2,1,0:T(4,128)}, u32[]{:S(2)}) copy-start(s32[16,4,8]{2,1,0:T(4,128)} %get-tuple-element.33) | copy-start | bytes 6148
  167.4 6.1 %copy-start.12 = (f32[16,4,8]{0,2,1:T(8,128)S(1)}, f32[16,4,8]{0,2,1:T(8,128)}, u32[]{:S(2)}) copy-start(f32[16,4,8]{0,2,1:T(8,128)} %param.18) | copy-start | bytes 6148
  167.4 58.2 %all-to-all-start.3 = ((bf16[128,8,2048]{2,1,0:T(8,128)(2,1)}), bf16[128,8,2048]{2,1,0:T(8,128)(2,1)}, u32[]{:S(2)}, u32[]{:S(2)}) async-start(bf16[128,8,2048]{2,1,0:T(8,128)(2,1)} %bitcast.50), calls=%async_computation.3 | async-start | bytes 8388608 | tf_op jit(solution)/shard_map/all_to_all | solution.py:469
